TPU v7x, 256 devices: a whole 4x4x8 slice. The times are simulated.
256 devices in a mesh: gx: 2 (over y_hi), gy: 16 (over z, y_lo), gz: 8 (over x, core).
Axes of the slice: x: 4, y: 4 (y_hi: 2, y_lo: 2; y = y_hi * 2 + y_lo), z: 8, core: 2. Of those that a mesh axis runs over, the one named last changes fastest.
Arguments:
- velocity: float32 [6, 128, 256, 1024], P(None, 'gx', 'gy', 'gz'), may hold values from -70 to 70, as said below
- basis_old: float32 [128, 96], P('gx'), may hold values from -0.5 to 0.5
- basis_mid: float32 [256, 96], P('gy'), may hold values from -0.375 to 0.375
- basis_deep: float32 [1024, 48], P('gz'), may hold values from -0.1875 to 0.1875
Outputs:
- basis_new: float32 [128, 96], P('gx')
- core_block: float32 [96, 48, 6, 96], P('gy', 'gz')
Inputs may be any that keep to these rules, and one draw needn't show every extreme that they name: A velocity field of order one with a few shared flow patterns.
All inputs are finite; a program needn't handle non-finite values.
Results may differ from a plain program's by a relative error of at most 0.0003.
Values sent between devices are 32-bit elements; how exact they have to be, the bound alone decides.
No kernel may reach another device: no remote copies, remote signals or barrier semaphores. Data moves between devices by JAX's collectives and lax.ppermute only.
A program may use at most 128 MiB of HBM per device.

v0:
```python
import jax
import jax.numpy as jnp
from jax import lax
from jax.sharding import PartitionSpec as P


def on_device(velocity, basis_old, basis_mid, basis_deep):
    high = lax.Precision.HIGHEST
    depth_groups = lax.axis_size("gz")
    width_groups = lax.axis_size("gy")
    deep_split = basis_deep.reshape(
        basis_deep.shape[0], depth_groups, basis_deep.shape[1] // depth_groups
    )
    mid_split = basis_mid.reshape(
        basis_mid.shape[0], width_groups, basis_mid.shape[1] // width_groups
    )
    partial_three = jnp.einsum("kabc,cRr->kabRr", velocity, deep_split, precision=high)
    partial_both = jnp.einsum("kabRr,bQq->QRqrka", partial_three, mid_split, precision=high)
    blocks = partial_both.reshape((width_groups * depth_groups,) + partial_both.shape[2:])
    projected = lax.psum_scatter(blocks, ("gy", "gz"), scatter_dimension=0, tiled=True)[0]
    mixing = lax.psum(jnp.einsum("qrka,aj->qrkj", projected, basis_old, precision=high), "gx")
    image = lax.psum(jnp.einsum("qrka,qrkj->aj", projected, mixing, precision=high), ("gy", "gz"))
    gram = lax.psum(jnp.dot(image.T, image, precision=high), "gx")
    lower = jnp.linalg.cholesky(gram)
    basis_new = lax.linalg.triangular_solve(
        lower, image, left_side=False, lower=True, transpose_a=True
    )
    core_block = lax.psum(jnp.einsum("aj,qrka->qrkj", basis_new, projected, precision=high), "gx")
    return (basis_new, core_block)


def solution(mesh):
    placed = (P(None, "gx", "gy", "gz"), P("gx", None), P("gy", None), P("gz", None))
    return jax.shard_map(
        on_device,
        mesh=mesh,
        in_specs=placed,
        out_specs=(P("gx", None), P("gy", "gz", None, None)),
        check_vma=False,
    )
```

profile of v0, /device:TPU:32, one launch (start us, length us, event | category | flops | bytes accessed | tf_op | source)
XLA Modules:
  0.0 1874.8 jit_solution(10667522108726989282)
XLA Ops:
  7.2 0.0 copy-start
  7.2 0.0 all-reduce.9.cloned.1.call-start
  7.2 0.9 reshape.22
  8.1 0.8 reshape.32
  8.9 0.2 copy.28
  9.1 0.0 copy-done
  9.1 27.9 %convolution_bitcast_fusion = f32[6,64,16,8,6,1]{2,3,4,1,0,5:T(8,128)S(1)} fusion(f32[6,64,16,128]{3,2,1,0:T(8,128)S(1)} %copy-done, f32[128,8,6,1,1]{0,2,1,4,3:T(8,128)S(1)} %bitcast.52), kind=kOutput, calls=%fused_computation.4 | convolution fusion | flops 452984832 | bytes 4349952 | tf_op jit(solution)/shard_map/kabc,cRr->kabRr/dot_general | solution.py:17
  37.0 30.0 %fusion.2 = f32[16,8,6,6,6,64]{5,0,2,3,1,4:T(8,128)} fusion(f32[16,16,6,1,1,1]{0,1,2,5,4,3:T(8,128)S(1)} %copy.28, f32[6,64,16,8,6,1]{2,3,4,1,0,5:T(8,128)S(1)} %convolution_bitcast_fusion), kind=kOutput, calls=%fused_computation.3 | convolution fusion | flops 339738624 | bytes 8263680 | tf_op jit(solution)/shard_map/kabRr,bQq->QRqrka/dot_general | solution.py:18
  67.1 18.3 copy.65
  85.3 0.0 copy-start.3
  85.3 0.0 copy-start.2
  85.3 0.0 all-reduce.9.cloned.1.call-update
  85.3 0.0 all-reduce.5.cloned.1.call-start
  85.4 0.6 copy-done.3
  86.0 0.6 dynamic-slice
  86.6 1097.1 %all-reduce.9.cloned.1.call-done = f32[128,6,6,6,64]{4,0,3,2,1:T(8,128)} async-done(((f32[128,6,6,6,64]{4,0,3,2,1:T(8,128)}), f32[128,6,6,6,64]{4,0,3,2,1:T(8,128)}) %all-reduce.9.cloned.1.call-update) | async-done | bytes 7077904
  1183.7 1.9 constant_dynamic-slice_fusion
  1185.6 0.0 copy-done.2
  1185.6 1.0 fusion.6
  1186.6 0.0 all-reduce.5.cloned.1.call-update
  1186.7 0.0 all-reduce.7.cloned.1.call-start
  1186.7 66.0 %all-reduce.5.cloned.1.call-done = f32[6,6,6,96]{3,1,0,2:T(8,128)} async-done(((f32[6,6,6,96]{3,1,0,2:T(8,128)}), f32[6,6,6,96]{3,1,0,2:T(8,128)}) %all-reduce.5.cloned.1.call-update) | async-done | bytes 82960 | tf_op jit(solution)/shard_map/psum | solution.py:21
  1252.7 1.3 convolution_bitcast_fusion.1
  1254.0 511.1 %psum.29 = f32[64,96]{1,0:T(8,128)S(1)} all-reduce(f32[64,96]{1,0:T(8,128)S(1)} %convolution_bitcast_fusion.1), channel_id=1, replica_groups=mesh['gx'=2,'gy'=16,'gz'=8] {'gy','gz'}, use_global_device_ids=true, to_apply=%region_2.0 | all-reduce | flops 6144 | bytes 49152 | tf_op jit(solution)/shard_map/psum | solution.py:22
  1765.1 0.3 fusion.22
  1765.4 10.9 psum.30
  1776.3 0.1 copy.24
  1776.4 8.8 cholesky.16
  1785.2 0.6 compare_reduce_fusion
  1785.8 0.7 fusion.15
  1786.5 7.4 custom-call.6
  1793.9 0.2 fusion.16
  1794.0 0.0 copy-start.1
  1794.0 1.0 fusion.10
  1795.1 0.0 all-reduce.7.cloned.1.call-update
  1795.1 71.4 %all-reduce.7.cloned.1.call-done = f32[6,6,6,96]{3,2,1,0:T(8,128)} async-done(((f32[6,6,6,96]{3,2,1,0:T(8,128)}), f32[6,6,6,96]{3,2,1,0:T(8,128)}) %all-reduce.7.cloned.1.call-update) | async-done | bytes 82960 | tf_op jit(solution)/shard_map/psum | solution.py:28
  1866.5 1.6 copy.69
  1868.0 0.0 copy-done.1
  (2 shorter events, 0.0 us)
Async XLA Ops:
  7.2 2.0 copy-start
  7.2 1176.5 %all-reduce.9.cloned.1.call-start = ((), (), s32[]{:S(2)}) async-start(), calls=%async_computation.2 | async-start | bytes 28311552
  85.3 0.7 copy-start.3
  85.3 1100.3 %copy-start.2 = (f32[64,96]{1,0:T(8,128)S(1)}, f32[64,96]{1,0:T(8,128)}, u32[]{:S(2)}) copy-start(f32[64,96]{1,0:T(8,128)} %param.5) | copy-start | bytes 73732
  85.3 1167.4 %all-reduce.5.cloned.1.call-start = ((), (), s32[]{:S(2)}) async-start(), calls=%async_computation | async-start | bytes 294912 | tf_op jit(solution)/shard_map/psum | solution.py:21
  1186.7 679.8 %all-reduce.7.cloned.1.call-start = ((), (), s32[]{:S(2)}) async-start(), calls=%async_computation.1 | async-start | bytes 294912 | tf_op jit(solution)/shard_map/psum | solution.py:28
  1794.0 74.0 %copy-start.1 = (f32[64,96]{1,0:T(8,128)}, f32[64,96]{1,0:T(8,128)S(1)}, u32[]{:S(2)}) copy-start(f32[64,96]{1,0:T(8,128)S(1)} %fusion.16) | copy-start | bytes 73732
Sparse Core Ops, SparseCore 0:
  85.5 1098.1 all-reduce.8
  1187.0 65.6 all-reduce.4
  1795.2 71.2 all-reduce.6
where the time goes:
time: 1880 us; the launch traced here: 1870 us
  waiting for transfers between devices  1230 us (65%)
  blocking collectives  522 us (28%)
  matrix products  61.7 us (3%)
  local copies, waits for them, and re-layouts  24.9 us (1%)
    unnamed x4, waiting for transfers between devices  1100 us
    psum x1, blocking collectives, on_device(): lax.psum(jnp.einsum('qrka,qrkj->aj', projected, mixing, precision=high),...  511 us
    psum x1, waiting for transfers between devices, on_device(): lax.psum(jnp.einsum('aj,qrka->qrkj', basis_new, projected, precision=high...  71.4 us
    psum x1, waiting for transfers between devices, on_device(): lax.psum(jnp.einsum('qrka,aj->qrkj', projected, basis_old, precision=high...  66 us
  transfers between devices with their start and end apart: 3, of which 3 were waited for; matrix products, arithmetic and copies ran while one was open for 0% of the time, Pallas kernels for 0%

commit v1 on v0

v1 whole, which is shorter than its diff:
```python
import functools

import jax
import jax.numpy as jnp
from jax import lax
from jax.experimental import pallas as pl
from jax.experimental.pallas import tpu as pltpu
from jax.sharding import Mesh, PartitionSpec as P

HIGH = lax.Precision.HIGHEST
F32 = jnp.float32
K, R1, NX = 6, 96, 128
XS, CORES, ZS, YS = 4, 2, 8, 4
PAIRS = 36
SLOTS = 5
TILES = 8


def dot(a, b, ca, cb):
    return lax.dot_general(a, b, (((ca,), (cb,)), ((), ())), precision=HIGH, preferred_element_type=F32)


def project_deep(vel_ref, deep_ref, send_ref, keep_ref):
    k = pl.program_id(0)
    me = lax.axis_index("x") * CORES + lax.axis_index("core")
    rows = []
    for core in (1, 0):
        for x in range(XS):
            rows.append(deep_ref[me ^ (x * CORES + core), :, :])
    deep = jnp.concatenate(rows, axis=0)
    for i in range(8):
        cells = jnp.concatenate([vel_ref[0, :, 2 * i, :], vel_ref[0, :, 2 * i + 1, :]], axis=0)
        part = dot(deep, cells, 1, 1)
        send_ref[pl.ds(k * 8 + i, 24, stride=48), :] = part[:24]
        keep_ref[pl.ds(k * 8 + i, 24, stride=48), :] = part[24:]


def pack_depth(a_ref, b_ref, c_ref, d_ref, mid_ref, old_ref, out_ref):
    z = lax.axis_index("z")
    source = lax.broadcasted_iota(jnp.int32, (R1, 128), 0)
    lane = lax.broadcasted_iota(jnp.int32, (R1, 128), 1)
    yl, zz, t = lane >> 6, (lane >> 3) & 7, lane & 7
    pick = jnp.where((source == (zz * 2 + yl) * 6 + t) & (t < 6), 1.0, 0.0).astype(F32)
    even = dot(mid_ref[pl.ds(0, 8, stride=2), :], pick, 1, 0)
    odd = dot(mid_ref[pl.ds(1, 8, stride=2), :], pick, 1, 0)
    old = jnp.concatenate([old_ref[pl.ds(pl.multiple_of(z * 8, 8), 8), :], jnp.zeros((8, 32), F32)], axis=1)
    for dest in range(ZS):
        for slot in range(SLOTS):
            pair = dest * SLOTS + slot
            if pair < PAIRS:
                at = pl.ds(pair * 8, 8)
                out_ref[dest, slot] = (a_ref[at, :] + b_ref[at, :]) + (c_ref[at, :] + d_ref[at, :])
            else:
                out_ref[dest, slot] = jnp.zeros((8, 128), F32)
        out_ref[dest, 5] = even
        out_ref[dest, 6] = odd
        out_ref[dest, 7] = old


def project_mid(r0, r1, r2, r3, image_ref, share_ref, whole):
    me = lax.axis_index("yh") * 2 + lax.axis_index("yl")
    for rel, ref in enumerate((r0, r1, r2, r3)):
        whole[me ^ rel] = ref[...]
    mids = []
    for yl in range(2):
        for par in range(2):
            mids.append(whole[yl, :, 5 + par].reshape(64, 128))
    mid = jnp.concatenate(mids, axis=0)
    mid_t = mid.T
    old = jnp.concatenate([whole[yh * 2, :, 7].reshape(64, 128) for yh in range(2)], axis=0)
    low = lax.broadcasted_iota(jnp.int32, (64, 128), 1) < 64
    parts = []
    for slot in range(SLOTS):
        rows = []
        for yl in range(2):
            first = whole[yl, :, slot].reshape(64, 128)
            second = whole[2 + yl, :, slot].reshape(64, 128)
            rows.append(jnp.where(low, first, pltpu.roll(second, 64, 1)))
            rows.append(jnp.where(low, pltpu.roll(first, 64, 1), second))
        parts.append(dot(mid_t, jnp.concatenate(rows, axis=0), 1, 0))
    yl = lax.axis_index("yl")
    for slot in range(SLOTS):
        half = jnp.where(yl == 0, parts[slot][:64], parts[slot][64:])
        for z in range(ZS):
            share_ref[z, slot] = half[z * 8:(z + 1) * 8]
    stack = jnp.concatenate(parts, axis=0)
    square = dot(stack, stack, 0, 0)
    image_ref[...] = dot(old[:, :R1], square, 0, 0)


def finish(p_ref, q_ref, share_ref, basis_ref, core_ref, rows_ref, turn_ref):
    image_t = p_ref[...] + q_ref[...]
    gram = dot(image_t, image_t, 1, 1)
    gram = jnp.concatenate([gram, jnp.zeros((R1, 128 - R1), F32)], axis=1)
    both = [jnp.concatenate([gram[8 * p:8 * p + 8], image_t[8 * p:8 * p + 8]], axis=1) for p in range(12)]
    row = lax.broadcasted_iota(jnp.int32, (8, 256), 0)
    done = []
    for p in range(12):
        d = both[p]
        for j in range(8):
            at = 8 * p + j
            col = d[:, at:at + 1]
            inv = lax.rsqrt(col[j:j + 1, :])
            pivot = d[j:j + 1, :] * inv
            d = jnp.where(row > j, d - (col * inv) * pivot, jnp.where(row == j, pivot, d))
        done.append(d[:, 128:])
        if p < 11:
            change = dot(d[:, :128], d, 0, 0)
            for r in range(p + 1, 12):
                both[r] = both[r] - change[8 * r:8 * r + 8]
    basis_t = jnp.concatenate(done, axis=0)
    turn_ref[...] = basis_t.T
    yh = lax.axis_index("yh")
    basis_ref[...] = turn_ref[pl.ds(pl.multiple_of(yh * 64, 64), 64), :]
    for t in range(6):
        for r in range(6):
            rows_ref[pl.ds((t * 6 + r) * 8, 6), :] = share_ref[pl.ds(r * 48 + t, 6, stride=8), :]
            rows_ref[pl.ds((t * 6 + r) * 8 + 6, 2), :] = jnp.zeros((2, 128), F32)
    core = dot(rows_ref[...], basis_t, 1, 1)
    core_ref[...] = core.reshape(6, 6, 8, R1)[:, :, :6, :]


VMEM = pl.BlockSpec(memory_space=pltpu.VMEM)


def call(kernel, outs, *args, scratch=()):
    return pl.pallas_call(
        kernel,
        out_shape=[jax.ShapeDtypeStruct(s, F32) for s in outs],
        in_specs=[VMEM] * len(args),
        out_specs=[VMEM] * len(outs),
        scratch_shapes=[pltpu.VMEM(s, F32) for s in scratch],
        compiler_params=pltpu.CompilerParams(vmem_limit_bytes=32 * 2**20),
    )(*args)


def swap(value, axis, size, bit):
    return lax.ppermute(value, axis, [(i, i ^ bit) for i in range(size)])


def on_device(velocity, basis_old, basis_mid, basis_deep):
    deep = basis_deep.T.reshape(8, 6, 128)
    rows = XS * PAIRS * 8
    send, keep = pl.pallas_call(
        project_deep,
        grid=(K,),
        out_shape=[jax.ShapeDtypeStruct((rows, 128), F32)] * 2,
        in_specs=[
            pl.BlockSpec((1, 64, 16, 128), lambda k: (k, 0, 0, 0)),
            pl.BlockSpec((8, 6, 128), lambda k: (0, 0, 0)),
        ],
        out_specs=[pl.BlockSpec((rows, 128), lambda k: (0, 0))] * 2,
        compiler_params=pltpu.CompilerParams(vmem_limit_bytes=32 * 2**20),
    )(velocity, deep)
    got = swap(send, "core", CORES, 1)
    keep, got = (v.reshape(XS, PAIRS * 8, 128) for v in (keep, got))
    sums = [keep[m] + got[m] for m in range(XS)]
    others = [swap(sums[m], "x", XS, m) for m in (2, 1, 3)]
    (packed,) = call(pack_depth, [(ZS, TILES, 8, 128)], sums[0], others[1], others[0], others[2], basis_mid, basis_old)
    mine = lax.all_to_all(packed, "z", 0, 0, tiled=True)
    near = {m: swap(mine, ("yh", "yl"), YS, m) for m in (2, 1, 3)}
    image, share = call(
        project_mid,
        [(R1, NX), (ZS, SLOTS, 8, 128)],
        mine, near[1], near[2], near[3],
        scratch=[(YS, ZS, TILES, 8, 128)],
    )
    shares = lax.all_to_all(share, "z", 0, 0, tiled=True)
    for axis, size, bit in (("core", 2, 1), ("x", 4, 1), ("x", 4, 3), ("z", 8, 1), ("z", 8, 2)):
        image = image + swap(image, axis, size, bit)
    last = swap(image, "z", 8, 7)
    basis_new, core_block = call(
        finish,
        [(64, R1), (6, 6, 6, R1)],
        image, last, shares.reshape(ZS * SLOTS * 8, 128),
        scratch=[(288, 128), (NX, R1)],
    )
    return (basis_new, core_block)


def solution(mesh):
    parts = Mesh(mesh.devices.reshape(2, 8, 2, 4, 2), ("yh", "z", "yl", "x", "core"))
    placed = (P(None, "yh", ("z", "yl"), ("x", "core")), P("yh", None), P(("z", "yl"), None), P(("x", "core"), None))
    return jax.shard_map(
        on_device,
        mesh=parts,
        in_specs=placed,
        out_specs=(P("yh", None), P(("z", "yl"), ("x", "core"), None, None)),
        check_vma=False,
    )
```

time: 1880 us -> 99.3 us (0.05)
  waiting for transfers between devices: 1230 us -> 32.4 us
  blocking collectives: 522 us -> 17.9 us
  matrix products: 61.7 us -> 0 us
  starting transfers between devices: 0.12 us -> 24.6 us
  local copies, waits for them, and re-layouts: 24.9 us -> 2.65 us
  Pallas kernels: 0 us -> 20.5 us
    unnamed x4 -> x0, waiting for transfers between devices: 1100 us -> none
    psum x2 -> x0, blocking collectives: 522 us -> none  [the longest x1 511 us: on_device(): lax.psum(jnp.einsum('qrka,qrkj->aj', projected, mixing, precision=high),...]
    psum x2 -> x0, waiting for transfers between devices: 137 us -> none  [the longest x1 71.4 us: on_device(): lax.psum(jnp.einsum('aj,qrka->qrkj', basis_new, projected, precision=high...]
    dot_general x6 -> x0, matrix products: 61.5 us -> none  [the longest x1 30 us: on_device(): jnp.einsum('kabRr,bQq->QRqrka', partial_three, mid_split, precision=high)]
    ppermute x0 -> x13, waiting for transfers between devices: none -> 32.4 us  [swap(): return lax.ppermute(value, axis, [(i, i ^ bit) for i in range(size)])]
    pallas_call x0 -> x4, Pallas kernels: none -> 20.5 us  [the longest x3 14.5 us: call(): pl.pallas_call(kernel, out_shape=[jax.ShapeDtypeStruct(s, F32) for s in o...]
    ppermute x0 -> x13, starting transfers between devices: none -> 19.4 us  [swap(): return lax.ppermute(value, axis, [(i, i ^ bit) for i in range(size)])]
  transfers between devices with their start and end apart: 3 -> 14, of which waited for: 3 -> 11; matrix products, arithmetic and copies ran while one was open for 0% -> 0% of each run, Pallas kernels for 0% -> 0%
where the time goes in v1:
time: 99.3 us; the launch traced here: 98.8 us
  waiting for transfers between devices  32.4 us (33%)
  starting transfers between devices  24.6 us (25%)
  Pallas kernels  20.5 us (21%)
  blocking collectives  17.9 us (18%)
  local copies, waits for them, and re-layouts  2.65 us (3%)
    ppermute x13, waiting for transfers between devices, swap(): return lax.ppermute(value, axis, [(i, i ^ bit) for i in range(size)])  32.4 us
    ppermute x13, starting transfers between devices, swap(): return lax.ppermute(value, axis, [(i, i ^ bit) for i in range(size)])  19.4 us
    all_to_all x1, blocking collectives, on_device(): mine = lax.all_to_all(packed, 'z', 0, 0, tiled=True)  17.9 us
    pallas_call x3, Pallas kernels, call(): pl.pallas_call(kernel, out_shape=[jax.ShapeDtypeStruct(s, F32) for s in o...  14.5 us
    pallas_call x1, Pallas kernels, on_device(): pl.pallas_call(project_deep, grid=(K,), out_shape=[jax.ShapeDtypeStruct((...  6.01 us
    all_to_all x1, starting transfers between devices, on_device(): shares = lax.all_to_all(share, 'z', 0, 0, tiled=True)  5.2 us
  transfers between devices with their start and end apart: 14, of which 11 were waited for; matrix products, arithmetic and copies ran while one was open for 0% of the time, Pallas kernels for 0%

profile of v1, /device:TPU:32, one launch (start us, length us, event | category | flops | bytes accessed | tf_op | source)
XLA Modules:
  0.0 98.8 jit_solution(7982960379367029821)
XLA Ops:
  0.6 0.0 copy-start.2
  0.6 0.0 copy-start.1
  0.7 0.8 reshape.28.deep_ref
  1.4 0.0 copy-start
  1.4 1.9 %copy-done = f32[6,64,16,128]{3,2,1,0:T(8,128)S(1)} copy-done((f32[6,64,16,128]{3,2,1,0:T(8,128)S(1)}, f32[6,64,16,128]{3,2,1,0:T(8,128)}, u32[]{:S(2)}) %copy-start) | copy-done | bytes 3145752
  3.3 6.0 %shard_map.59 = (f32[1152,128]{1,0:T(8,128)S(1)}, f32[1152,128]{1,0:T(8,128)S(1)}) custom-call(f32[6,64,16,128]{3,2,1,0:T(8,128)S(1)} %copy-done, f32[8,6,128]{2,1,0:T(8,128)S(1)} %reshape.28.deep_ref), custom_call_target="tpu_custom_call" | custom-call | tf_op jit(solution)/shard_map/pallas_call | solution.py:144
  9.3 0.1 collective-permute-start
  9.4 2.0 %collective-permute-done = f32[1152,128]{1,0:T(8,128)S(1)} collective-permute-done((f32[1152,128]{1,0:T(8,128)S(1)}, f32[1152,128]{1,0:T(8,128)S(1)}, u32[]{:S(2)}, u32[]{:S(2)}) %collective-permute-start) | collective-permute-done | bytes 589856 | tf_op jit(solution)/shard_map/ppermute | solution.py:138
  11.4 0.1 slice_add_fusion
  11.5 2.8 %collective-permute-start.3 = (f32[288,128]{1,0:T(8,128)S(1)}, f32[288,128]{1,0:T(8,128)S(1)}, u32[]{:S(2)}, u32[]{:S(2)}) collective-permute-start(f32[288,128]{1,0:T(8,128)S(1)} %get-tuple-element.10), channel_id=1, source_target_pairs={{0,6},{2,4},{4,2},{6,0},{1,7},{3,5},{5,3},{7,1},{8,14},{10,12},{12... | collective-permute-start | bytes 442376 | tf_op jit(solution)/shard_map/ppermute | solution.py:138
  14.3 0.8 collective-permute-start.2
  15.1 0.5 collective-permute-start.1
  15.6 5.4 %collective-permute-done.3.d_ref = f32[288,128]{1,0:T(8,128)S(1)} collective-permute-done((f32[288,128]{1,0:T(8,128)S(1)}, f32[288,128]{1,0:T(8,128)S(1)}, u32[]{:S(2)}, u32[]{:S(2)}) %collective-permute-start.3) | collective-permute-done | bytes 147488 | tf_op jit(solution)/shard_map/ppermute | solution.py:138
  21.1 1.5 %collective-permute-done.2.c_ref = f32[288,128]{1,0:T(8,128)S(1)} collective-permute-done((f32[288,128]{1,0:T(8,128)S(1)}, f32[288,128]{1,0:T(8,128)S(1)}, u32[]{:S(2)}, u32[]{:S(2)}) %collective-permute-start.2) | collective-permute-done | bytes 147488 | tf_op jit(solution)/shard_map/ppermute | solution.py:138
  22.5 0.0 collective-permute-done.1.b_ref
  22.5 0.0 copy-done.2
  22.6 0.0 copy-done.1
  22.6 0.2 shard_map.60
  22.8 17.9 %all_to_all.10.r0 = f32[8,8,8,128]{3,2,1,0:T(8,128)S(1)} all-to-all(f32[8,8,8,128]{3,2,1,0:T(8,128)S(1)} %shard_map.60), channel_id=1, replica_groups=mesh['yh'=2,'z'=8,'yl'=2,'x'=4,'core'=2] {'z'}, dimensions={0} | all-to-all | bytes 524288 | tf_op jit(solution)/shard_map/all_to_all | solution.py:160
  40.6 3.0 %collective-permute-start.6 = (f32[8,8,8,128]{3,2,1,0:T(8,128)S(1)}, f32[8,8,8,128]{3,2,1,0:T(8,128)S(1)}, u32[]{:S(2)}, u32[]{:S(2)}) collective-permute-start(f32[8,8,8,128]{3,2,1,0:T(8,128)S(1)} %all_to_all.10.r0), channel_id=1, source_target_pairs={{0,136},{8,128},{128,8},{136,0},{1,137},{9,129},{129,9},{137,1},{2... | collective-permute-start | bytes 786440 | tf_op jit(solution)/shard_map/ppermute | solution.py:138
  43.7 0.6 collective-permute-start.5
  44.3 0.5 collective-permute-start.4
  44.7 7.0 %collective-permute-done.6.r3 = f32[8,8,8,128]{3,2,1,0:T(8,128)S(1)} collective-permute-done((f32[8,8,8,128]{3,2,1,0:T(8,128)S(1)}, f32[8,8,8,128]{3,2,1,0:T(8,128)S(1)}, u32[]{:S(2)}, u32[]{:S(2)}) %collective-permute-start.6) | collective-permute-done | bytes 262176 | tf_op jit(solution)/shard_map/ppermute | solution.py:138
  51.7 0.9 collective-permute-done.5.r2
  52.6 0.5 collective-permute-done.4.r1
  53.1 1.6 %shard_map.61 = (f32[96,128]{1,0:T(8,128)S(1)}, f32[8,5,8,128]{3,2,1,0:T(8,128)}) custom-call(f32[8,8,8,128]{3,2,1,0:T(8,128)S(1)} %all_to_all.10.r0, f32[8,8,8,128]{3,2,1,0:T(8,128)S(1)} %collective-permute-done.4.r1, f32[8,8,8,128]{3,2,1,0:T(8,128)S(1)} %collective-permute-done.5.r2, f32[8,8,8,128]{3,2,1,0:T(8,128)S(1)} %collective-permute-done.6.r3), custom_call_target="tpu_custom_call" | custom-call | tf_op jit(solution)/shard_map/pallas_call | solution.py:127
  54.7 0.0 collective-permute-start.7
  54.7 5.2 %all-to-all-start.1 = ((f32[8,5,8,128]{3,2,1,0:T(8,128)}), f32[8,5,8,128]{3,2,1,0:T(8,128)S(1)}, u32[]{:S(2)}, u32[]{:S(2)}) async-start(f32[8,5,8,128]{3,2,1,0:T(8,128)} %get-tuple-element.9), calls=%async_computation.1 | async-start | bytes 327680 | tf_op jit(solution)/shard_map/all_to_all | solution.py:168
  59.9 0.0 collective-permute-done.7
  59.9 1.7 %collective-permute-start.8 = (f32[96,128]{1,0:T(8,128)S(1)}, f32[96,128]{1,0:T(8,128)S(1)}, u32[]{:S(2)}, u32[]{:S(2)}) collective-permute-start(f32[96,128]{1,0:T(8,128)S(1)} %add.31), channel_id=1, source_target_pairs={{0,2},{2,0},{4,6},{6,4},{1,3},{3,1},{5,7},{7,5},{8,10},{10,8},{12,... | collective-permute-start | bytes 147464 | tf_op jit(solution)/shard_map/ppermute | solution.py:138
  61.6 2.5 %collective-permute-done.8 = f32[96,128]{1,0:T(8,128)S(1)} collective-permute-done((f32[96,128]{1,0:T(8,128)S(1)}, f32[96,128]{1,0:T(8,128)S(1)}, u32[]{:S(2)}, u32[]{:S(2)}) %collective-permute-start.8) | collective-permute-done | bytes 49184 | tf_op jit(solution)/shard_map/ppermute | solution.py:138
  64.1 3.0 %collective-permute-start.9 = (f32[96,128]{1,0:T(8,128)S(1)}, f32[96,128]{1,0:T(8,128)S(1)}, u32[]{:S(2)}, u32[]{:S(2)}) collective-permute-start(f32[96,128]{1,0:T(8,128)S(1)} %add.32), channel_id=1, source_target_pairs={{0,6},{2,4},{4,2},{6,0},{1,7},{3,5},{5,3},{7,1},{8,14},{10,12},{12... | collective-permute-start | bytes 147464 | tf_op jit(solution)/shard_map/ppermute | solution.py:138
  67.1 2.4 %collective-permute-done.9 = f32[96,128]{1,0:T(8,128)S(1)} collective-permute-done((f32[96,128]{1,0:T(8,128)S(1)}, f32[96,128]{1,0:T(8,128)S(1)}, u32[]{:S(2)}, u32[]{:S(2)}) %collective-permute-start.9) | collective-permute-done | bytes 49184 | tf_op jit(solution)/shard_map/ppermute | solution.py:138
  69.5 0.1 collective-permute-start.10
  69.6 4.1 %collective-permute-done.10 = f32[96,128]{1,0:T(8,128)S(1)} collective-permute-done((f32[96,128]{1,0:T(8,128)S(1)}, f32[96,128]{1,0:T(8,128)S(1)}, u32[]{:S(2)}, u32[]{:S(2)}) %collective-permute-start.10) | collective-permute-done | bytes 49184 | tf_op jit(solution)/shard_map/ppermute | solution.py:138
  73.7 2.4 %collective-permute-start.11 = (f32[96,128]{1,0:T(8,128)S(1)}, f32[96,128]{1,0:T(8,128)S(1)}, u32[]{:S(2)}, u32[]{:S(2)}) collective-permute-start(f32[96,128]{1,0:T(8,128)S(1)} %add.34), channel_id=1, source_target_pairs={{0,32},{16,48},{32,0},{48,16},{64,96},{80,112},{96,64},{112,80},{1... | collective-permute-start | bytes 147464 | tf_op jit(solution)/shard_map/ppermute | solution.py:138
  76.1 2.6 %collective-permute-done.11 = f32[96,128]{1,0:T(8,128)S(1)} collective-permute-done((f32[96,128]{1,0:T(8,128)S(1)}, f32[96,128]{1,0:T(8,128)S(1)}, u32[]{:S(2)}, u32[]{:S(2)}) %collective-permute-start.11) | collective-permute-done | bytes 49184 | tf_op jit(solution)/shard_map/ppermute | solution.py:138
  78.8 3.8 %collective-permute-start.12 = (f32[96,128]{1,0:T(8,128)S(1)}, f32[96,128]{1,0:T(8,128)S(1)}, u32[]{:S(2)}, u32[]{:S(2)}) collective-permute-start(f32[96,128]{1,0:T(8,128)S(1)} %add.35.p_ref), channel_id=1, source_target_pairs={{0,112},{16,96},{32,80},{48,64},{64,48},{80,32},{96,16},{112,0},{1... | collective-permute-start | bytes 147464 | tf_op jit(solution)/shard_map/ppermute | solution.py:138
  82.6 0.0 all-to-all-done.1
  82.6 3.5 %collective-permute-done.12.q_ref = f32[96,128]{1,0:T(8,128)S(1)} collective-permute-done((f32[96,128]{1,0:T(8,128)S(1)}, f32[96,128]{1,0:T(8,128)S(1)}, u32[]{:S(2)}, u32[]{:S(2)}) %collective-permute-start.12) | collective-permute-done | bytes 49184 | tf_op jit(solution)/shard_map/ppermute | solution.py:138
  86.1 12.7 %shard_map.62 = (f32[64,96]{1,0:T(8,128)}, f32[6,6,6,96]{3,2,1,0:T(8,128)}) custom-call(f32[96,128]{1,0:T(8,128)S(1)} %add.35.p_ref, f32[96,128]{1,0:T(8,128)S(1)} %collective-permute-done.12.q_ref, f32[320,128]{1,0:T(8,128)S(1)} %bitcast.2), custom_call_target="tpu_custom_call" | custom-call | tf_op jit(solution)/shard_map/pallas_call | solution.py:127
  (5 shorter events, 0.0 us)
Async XLA Ops:
  0.6 21.9 %copy-start.2 = (f32[16,96]{1,0:T(8,128)S(1)}, f32[16,96]{1,0:T(8,128)}, u32[]{:S(2)}) copy-start(f32[16,96]{1,0:T(8,128)} %mid_ref.1) | copy-start | bytes 18436
  0.6 21.9 %copy-start.1 = (f32[64,96]{1,0:T(8,128)S(1)}, f32[64,96]{1,0:T(8,128)}, u32[]{:S(2)}) copy-start(f32[64,96]{1,0:T(8,128)} %old_ref.1) | copy-start | bytes 73732
  1.4 1.9 %copy-start = (f32[6,64,16,128]{3,2,1,0:T(8,128)S(1)}, f32[6,64,16,128]{3,2,1,0:T(8,128)}, u32[]{:S(2)}) copy-start(f32[6,64,16,128]{3,2,1,0:T(8,128)} %vel_ref.1) | copy-start | bytes 9437188
  9.3 2.1 %collective-permute-start = (f32[1152,128]{1,0:T(8,128)S(1)}, f32[1152,128]{1,0:T(8,128)S(1)}, u32[]{:S(2)}, u32[]{:S(2)}) collective-permute-start(f32[1152,128]{1,0:T(8,128)S(1)} %get-tuple-element.7), channel_id=1, source_target_pairs={{0,1},{1,0},{2,3},{3,2},{4,5},{5,4},{6,7},{7,6},{8,9},{9,8},{10,11... | collective-permute-start | bytes 1769480 | tf_op jit(solution)/shard_map/ppermute | solution.py:138
  11.5 9.6 %collective-permute-start.3 = (f32[288,128]{1,0:T(8,128)S(1)}, f32[288,128]{1,0:T(8,128)S(1)}, u32[]{:S(2)}, u32[]{:S(2)}) collective-permute-start(f32[288,128]{1,0:T(8,128)S(1)} %get-tuple-element.10), channel_id=1, source_target_pairs={{0,6},{2,4},{4,2},{6,0},{1,7},{3,5},{5,3},{7,1},{8,14},{10,12},{12... | collective-permute-start | bytes 442376 | tf_op jit(solution)/shard_map/ppermute | solution.py:138
  14.3 8.2 %collective-permute-start.2 = (f32[288,128]{1,0:T(8,128)S(1)}, f32[288,128]{1,0:T(8,128)S(1)}, u32[]{:S(2)}, u32[]{:S(2)}) collective-permute-start(f32[288,128]{1,0:T(8,128)S(1)} %get-tuple-element.11), channel_id=1, source_target_pairs={{0,4},{2,6},{4,0},{6,2},{1,5},{3,7},{5,1},{7,3},{8,12},{10,14},{12... | collective-permute-start | bytes 442376 | tf_op jit(solution)/shard_map/ppermute | solution.py:138
  15.1 7.4 %collective-permute-start.1 = (f32[288,128]{1,0:T(8,128)S(1)}, f32[288,128]{1,0:T(8,128)S(1)}, u32[]{:S(2)}, u32[]{:S(2)}) collective-permute-start(f32[288,128]{1,0:T(8,128)S(1)} %get-tuple-element.12), channel_id=1, source_target_pairs={{0,2},{2,0},{4,6},{6,4},{1,3},{3,1},{5,7},{7,5},{8,10},{10,8},{12,... | collective-permute-start | bytes 442376 | tf_op jit(solution)/shard_map/ppermute | solution.py:138
  40.6 11.1 %collective-permute-start.6 = (f32[8,8,8,128]{3,2,1,0:T(8,128)S(1)}, f32[8,8,8,128]{3,2,1,0:T(8,128)S(1)}, u32[]{:S(2)}, u32[]{:S(2)}) collective-permute-start(f32[8,8,8,128]{3,2,1,0:T(8,128)S(1)} %all_to_all.10.r0), channel_id=1, source_target_pairs={{0,136},{8,128},{128,8},{136,0},{1,137},{9,129},{129,9},{137,1},{2... | collective-permute-start | bytes 786440 | tf_op jit(solution)/shard_map/ppermute | solution.py:138
  43.7 9.0 %collective-permute-start.5 = (f32[8,8,8,128]{3,2,1,0:T(8,128)S(1)}, f32[8,8,8,128]{3,2,1,0:T(8,128)S(1)}, u32[]{:S(2)}, u32[]{:S(2)}) collective-permute-start(f32[8,8,8,128]{3,2,1,0:T(8,128)S(1)} %all_to_all.10.r0), channel_id=1, source_target_pairs={{0,128},{8,136},{128,0},{136,8},{1,129},{9,137},{129,1},{137,9},{2... | collective-permute-start | bytes 786440 | tf_op jit(solution)/shard_map/ppermute | solution.py:138
  44.3 8.9 %collective-permute-start.4 = (f32[8,8,8,128]{3,2,1,0:T(8,128)S(1)}, f32[8,8,8,128]{3,2,1,0:T(8,128)S(1)}, u32[]{:S(2)}, u32[]{:S(2)}) collective-permute-start(f32[8,8,8,128]{3,2,1,0:T(8,128)S(1)} %all_to_all.10.r0), channel_id=1, source_target_pairs={{0,8},{8,0},{128,136},{136,128},{1,9},{9,1},{129,137},{137,129},{2... | collective-permute-start | bytes 786440 | tf_op jit(solution)/shard_map/ppermute | solution.py:138
  54.7 5.2 %collective-permute-start.7 = (f32[96,128]{1,0:T(8,128)S(1)}, f32[96,128]{1,0:T(8,128)S(1)}, u32[]{:S(2)}, u32[]{:S(2)}) collective-permute-start(f32[96,128]{1,0:T(8,128)S(1)} %get-tuple-element.8), channel_id=1, source_target_pairs={{0,1},{1,0},{2,3},{3,2},{4,5},{5,4},{6,7},{7,6},{8,9},{9,8},{10,11... | collective-permute-start | bytes 147464 | tf_op jit(solution)/shard_map/ppermute | solution.py:138
  54.7 27.9 %all-to-all-start.1 = ((f32[8,5,8,128]{3,2,1,0:T(8,128)}), f32[8,5,8,128]{3,2,1,0:T(8,128)S(1)}, u32[]{:S(2)}, u32[]{:S(2)}) async-start(f32[8,5,8,128]{3,2,1,0:T(8,128)} %get-tuple-element.9), calls=%async_computation.1 | async-start | bytes 327680 | tf_op jit(solution)/shard_map/all_to_all | solution.py:168
  59.9 4.2 %collective-permute-start.8 = (f32[96,128]{1,0:T(8,128)S(1)}, f32[96,128]{1,0:T(8,128)S(1)}, u32[]{:S(2)}, u32[]{:S(2)}) collective-permute-start(f32[96,128]{1,0:T(8,128)S(1)} %add.31), channel_id=1, source_target_pairs={{0,2},{2,0},{4,6},{6,4},{1,3},{3,1},{5,7},{7,5},{8,10},{10,8},{12,... | collective-permute-start | bytes 147464 | tf_op jit(solution)/shard_map/ppermute | solution.py:138
  64.1 5.4 %collective-permute-start.9 = (f32[96,128]{1,0:T(8,128)S(1)}, f32[96,128]{1,0:T(8,128)S(1)}, u32[]{:S(2)}, u32[]{:S(2)}) collective-permute-start(f32[96,128]{1,0:T(8,128)S(1)} %add.32), channel_id=1, source_target_pairs={{0,6},{2,4},{4,2},{6,0},{1,7},{3,5},{5,3},{7,1},{8,14},{10,12},{12... | collective-permute-start | bytes 147464 | tf_op jit(solution)/shard_map/ppermute | solution.py:138
  69.5 4.2 %collective-permute-start.10 = (f32[96,128]{1,0:T(8,128)S(1)}, f32[96,128]{1,0:T(8,128)S(1)}, u32[]{:S(2)}, u32[]{:S(2)}) collective-permute-start(f32[96,128]{1,0:T(8,128)S(1)} %add.33), channel_id=1, source_target_pairs={{0,16},{16,0},{32,48},{48,32},{64,80},{80,64},{96,112},{112,96},{1... | collective-permute-start | bytes 147464 | tf_op jit(solution)/shard_map/ppermute | solution.py:138
  73.7 5.1 %collective-permute-start.11 = (f32[96,128]{1,0:T(8,128)S(1)}, f32[96,128]{1,0:T(8,128)S(1)}, u32[]{:S(2)}, u32[]{:S(2)}) collective-permute-start(f32[96,128]{1,0:T(8,128)S(1)} %add.34), channel_id=1, source_target_pairs={{0,32},{16,48},{32,0},{48,16},{64,96},{80,112},{96,64},{112,80},{1... | collective-permute-start | bytes 147464 | tf_op jit(solution)/shard_map/ppermute | solution.py:138
  78.8 7.4 %collective-permute-start.12 = (f32[96,128]{1,0:T(8,128)S(1)}, f32[96,128]{1,0:T(8,128)S(1)}, u32[]{:S(2)}, u32[]{:S(2)}) collective-permute-start(f32[96,128]{1,0:T(8,128)S(1)} %add.35.p_ref), channel_id=1, source_target_pairs={{0,112},{16,96},{32,80},{48,64},{64,48},{80,32},{96,16},{112,0},{1... | collective-permute-start | bytes 147464 | tf_op jit(solution)/shard_map/ppermute | solution.py:138

commit v2 on v1

v2 whole, which is shorter than its diff:
```python
import jax
import jax.numpy as jnp
from jax import lax
from jax.experimental import pallas as pl
from jax.experimental.pallas import tpu as pltpu
from jax.sharding import Mesh, PartitionSpec as P

HIGH = lax.Precision.HIGHEST
F32, BF16 = jnp.float32, jnp.bfloat16
K, R1, NX = 6, 96, 128
XS, CORES, ZS, YS = 4, 2, 8, 4
PAIRS = 36
SLOTS = 5
TILES = 7
HALF = SLOTS * 48


def dot(a, b, ca, cb, precision=HIGH):
    return lax.dot_general(a, b, (((ca,), (cb,)), ((), ())), precision=precision, preferred_element_type=F32)


def halves(value):
    high = value.astype(BF16)
    return high, (value - high.astype(F32)).astype(BF16)


def project_deep(vel_ref, deep_ref, send_ref, keep_ref, cells_ref, sems):
    copies = [pltpu.make_async_copy(vel_ref.at[k], cells_ref.at[k], sems.at[k]) for k in range(K)]
    for copy in copies:
        copy.start()
    me = lax.axis_index("x") * CORES + lax.axis_index("core")
    rows = [deep_ref[me ^ (x * CORES + core)] for core in (1, 0) for x in range(XS)]
    high, low = halves(jnp.concatenate(rows, axis=0))
    deep = jnp.concatenate([jnp.concatenate([high, high], axis=1), jnp.concatenate([low, low], axis=1)], axis=0)
    for k in range(K):
        copies[k].wait()
        for i in range(0, 8, 2):
            cells = jnp.concatenate([cells_ref[k, :, b, :] for b in range(2 * i, 2 * i + 4)], axis=0)
            part = dot(deep, jnp.concatenate(halves(cells), axis=1), 1, 1, None)
            part = part[:48] + part[48:]
            for s in range(2):
                at = pl.ds(k * 8 + i + s, 24, stride=48)
                send_ref[at, :] = part[:24, s * 128:s * 128 + 128]
                keep_ref[at, :] = part[24:, s * 128:s * 128 + 128]


def pack_depth(a_ref, b_ref, c_ref, d_ref, mid_ref, out_ref):
    source = lax.broadcasted_iota(jnp.int32, (R1, 128), 0)
    lane = lax.broadcasted_iota(jnp.int32, (R1, 128), 1)
    yl = jnp.where(lane >= 48, 1, 0)
    at = lane - 48 * yl
    z = ((at.astype(F32) + 0.5) * (1.0 / 6.0)).astype(jnp.int32)
    pick = jnp.where((source == at + 6 * z + 6 * yl) & (lane < R1), 1.0, 0.0).astype(F32)
    even = dot(mid_ref[pl.ds(0, 8, stride=2), :], pick, 1, 0)
    odd = dot(mid_ref[pl.ds(1, 8, stride=2), :], pick, 1, 0)
    for dest in range(ZS):
        for slot in range(SLOTS):
            pair = dest * SLOTS + slot
            if pair < PAIRS:
                at = pl.ds(pair * 8, 8)
                out_ref[dest, slot] = (a_ref[at, :] + b_ref[at, :]) + (c_ref[at, :] + d_ref[at, :])
            else:
                out_ref[dest, slot] = jnp.zeros((8, 128), F32)
        out_ref[dest, 5] = even
        out_ref[dest, 6] = odd


def project_mid(got_ref, old_ref, part_ref, more_ref):
    mid = jnp.concatenate([got_ref[:, 5 + par].reshape(64, 128).T[:R1] for par in range(2)], axis=0)
    cells = jnp.concatenate([got_ref[:, slot].reshape(64, 128) for slot in range(SLOTS)], axis=1)
    both = dot(mid, cells, 1, 0)
    low = lax.broadcasted_iota(jnp.int32, (48, 128), 1) < 64
    for slot in range(SLOTS):
        at = slice(slot * 128, slot * 128 + 128)
        e0, e1, o0, o1 = (both[r * 48:r * 48 + 48, at] for r in range(4))
        first = e0 + pltpu.roll(o0, 64, 1)
        second = pltpu.roll(e1, 64, 1) + o1
        out = jnp.where(low, first, second)
        part_ref[slot * 48:slot * 48 + 48, :] = out
        more_ref[slot * 48:slot * 48 + 48, :] = out
    more_ref[HALF:HALF + 64, :] = jnp.concatenate([old_ref[...], jnp.zeros((64, 128 - R1), F32)], axis=1)


def form_image(own_ref, r1, r2, r3, old_ref, image_ref, share_ref):
    yh, yl = lax.axis_index("yh"), lax.axis_index("yl")
    near = own_ref[...] + r1[...]
    far = r2[:HALF, :] + r3[...]
    h0 = jnp.where(yh == 0, near, far)
    h1 = jnp.where(yh == 0, far, near)
    low = lax.broadcasted_iota(jnp.int32, (HALF, 128), 1) < 64
    p0 = jnp.where(low, h0, pltpu.roll(h1, 64, 1))
    p1 = jnp.where(low, pltpu.roll(h0, 64, 1), h1)
    mine = jnp.where(yl == 0, p0, p1)
    for slot in range(SLOTS):
        for z in range(ZS):
            share_ref[z, slot, 0:6, :] = mine[slot * 48 + z * 6:slot * 48 + z * 6 + 6]
    stack = jnp.concatenate([p0, p1], axis=0)
    square = dot(stack, stack, 0, 0)
    other = r2[HALF:HALF + 64, :R1]
    own = old_ref[...]
    old = jnp.concatenate([jnp.where(yh == 0, own, other), jnp.where(yh == 0, other, own)], axis=0)
    image_ref[...] = dot(old, square, 0, 0)


def solve(gram, image_t):
    size = 32
    count = R1 // size
    gram = jnp.concatenate([gram, jnp.zeros((R1, 128 - R1), F32)], axis=1)
    left = [gram[size * p:size * p + size] for p in range(count)]
    right = [image_t[size * p:size * p + size] for p in range(count)]
    row = lax.broadcasted_iota(jnp.int32, (size, 128), 0)
    done = []
    for p in range(count):
        a, x = left[p], right[p]
        columns = [jnp.broadcast_to(a[:, size * p + j:size * p + j + 1], (size, 128)) for j in range(size)]
        for j in range(size):
            inv = lax.rsqrt(columns[j][j:j + 1, :])
            m = columns[j] * inv
            for i in range(j + 1, size):
                columns[i] = columns[i] - m * m[i:i + 1, :]
            pa, px = a[j:j + 1, :] * inv, x[j:j + 1, :] * inv
            a = jnp.where(row > j, a - m * pa, jnp.where(row == j, pa, a))
            x = jnp.where(row > j, x - m * px, jnp.where(row == j, px, x))
        done.append(x)
        if p < count - 1:
            change = dot(a.T[size * (p + 1):R1], jnp.concatenate([a, x], axis=1), 1, 0)
            for r in range(p + 1, count):
                at = size * (r - p - 1)
                left[r] = left[r] - change[at:at + size, :128]
                right[r] = right[r] - change[at:at + size, 128:]
    return jnp.concatenate(done, axis=0)


def finish(p_ref, q_ref, share_ref, basis_ref, core_ref, rows_ref, turn_ref):
    image_t = p_ref[...] + q_ref[...]
    basis_t = solve(dot(image_t, image_t, 1, 1), image_t)
    turn_ref[...] = basis_t.T
    yh = lax.axis_index("yh")
    basis_ref[...] = turn_ref[pl.ds(pl.multiple_of(yh * 64, 64), 64), :]
    for t in range(6):
        for r in range(6):
            rows_ref[pl.ds((t * 6 + r) * 8, 6), :] = share_ref[pl.ds(r * 48 + t, 6, stride=8), :]
            rows_ref[pl.ds((t * 6 + r) * 8 + 6, 2), :] = jnp.zeros((2, 128), F32)
    core = dot(rows_ref[...], basis_t, 1, 1)
    core_ref[...] = core.reshape(6, 6, 8, R1)[:, :, :6, :]


VMEM = pl.BlockSpec(memory_space=pltpu.VMEM)


def call(kernel, outs, *args, scratch=()):
    return pl.pallas_call(
        kernel,
        out_shape=[jax.ShapeDtypeStruct(s, F32) for s in outs],
        in_specs=[VMEM] * len(args),
        out_specs=[VMEM] * len(outs),
        scratch_shapes=[pltpu.VMEM(s, F32) for s in scratch],
        compiler_params=pltpu.CompilerParams(vmem_limit_bytes=32 * 2**20),
    )(*args)


def swap(value, axis, size, bit):
    return lax.ppermute(value, axis, [(i, i ^ bit) for i in range(size)])


def on_device(velocity, basis_old, basis_mid, basis_deep):
    deep = basis_deep.T.reshape(8, 6, 128)
    rows = XS * PAIRS * 8
    send, keep = pl.pallas_call(
        project_deep,
        out_shape=[jax.ShapeDtypeStruct((rows, 128), F32)] * 2,
        in_specs=[pl.BlockSpec(memory_space=pltpu.HBM), VMEM],
        out_specs=[VMEM] * 2,
        scratch_shapes=[pltpu.VMEM((K, 64, 16, 128), F32), pltpu.SemaphoreType.DMA((K,))],
        compiler_params=pltpu.CompilerParams(vmem_limit_bytes=32 * 2**20),
    )(velocity, deep)
    got = swap(send, "core", CORES, 1)
    keep, got = (v.reshape(XS, PAIRS * 8, 128) for v in (keep, got))
    sums = [keep[m] + got[m] for m in range(XS)]
    others = {m: swap(sums[m], "x", XS, m) for m in (3, 1, 2)}
    (packed,) = call(pack_depth, [(ZS, TILES, 8, 128)], sums[0], others[1], others[2], others[3], basis_mid)
    mine = lax.all_to_all(packed, "z", 0, 0, tiled=True)
    part, more = call(project_mid, [(HALF, 128), (HALF + 64, 128)], mine, basis_old)
    near = {m: swap(more if m == 2 else part, ("yh", "yl"), YS, m) for m in (3, 1, 2)}
    image, share = call(
        form_image, [(R1, NX), (ZS, SLOTS, 8, 128)], part, near[1], near[2], near[3], basis_old
    )
    shares = lax.all_to_all(share, "z", 0, 0, tiled=True)
    for axis, size, bit in (("core", 2, 1), ("x", 4, 1), ("x", 4, 3), ("z", 8, 1), ("z", 8, 2)):
        image = image + swap(image, axis, size, bit)
    last = swap(image, "z", 8, 7)
    basis_new, core_block = call(
        finish,
        [(64, R1), (6, 6, 6, R1)],
        image, last, shares.reshape(ZS * SLOTS * 8, 128),
        scratch=[(288, 128), (NX, R1)],
    )
    return (basis_new, core_block)


def solution(mesh):
    parts = Mesh(mesh.devices.reshape(2, 8, 2, 4, 2), ("yh", "z", "yl", "x", "core"))
    placed = (P(None, "yh", ("z", "yl"), ("x", "core")), P("yh", None), P(("z", "yl"), None), P(("x", "core"), None))
    return jax.shard_map(
        on_device,
        mesh=parts,
        in_specs=placed,
        out_specs=(P("yh", None), P(("z", "yl"), ("x", "core"), None, None)),
        check_vma=False,
    )
```

time: 99.3 us -> 82.8 us (0.83)
  Pallas kernels: 20.5 us -> 8.47 us
  waiting for transfers between devices: 32.4 us -> 29.1 us
    pallas_call x3 -> x4, Pallas kernels: 14.5 us -> 5.31 us  [call(): pl.pallas_call(kernel, out_shape=[jax.ShapeDtypeStruct(s, F32) for s in o...]
    ppermute x13, waiting for transfers between devices: 32.4 us -> 29.1 us  [swap(): return lax.ppermute(value, axis, [(i, i ^ bit) for i in range(size)])]
    pallas_call x1, Pallas kernels: 6.01 us -> 3.17 us  [on_device(): pl.pallas_call(project_deep, out_shape=[jax.ShapeDtypeStruct((rows, 128),...]
  transfers between devices with their start and end apart: 14 -> 14, of which waited for: 11 -> 9; matrix products, arithmetic and copies ran while one was open for 0% -> 0% of each run, Pallas kernels for 0% -> 0%
where the time goes in v2:
time: 82.8 us; the launch traced here: 82.5 us
  waiting for transfers between devices  29.1 us (35%)
  starting transfers between devices  24.2 us (29%)
  blocking collectives  17.2 us (21%)
  Pallas kernels  8.47 us (10%)
  local copies, waits for them, and re-layouts  2.65 us (3%)
    ppermute x13, waiting for transfers between devices, swap(): return lax.ppermute(value, axis, [(i, i ^ bit) for i in range(size)])  29.1 us
    ppermute x13, starting transfers between devices, swap(): return lax.ppermute(value, axis, [(i, i ^ bit) for i in range(size)])  19.4 us
    all_to_all x1, blocking collectives, on_device(): mine = lax.all_to_all(packed, 'z', 0, 0, tiled=True)  17.2 us
    pallas_call x4, Pallas kernels, call(): pl.pallas_call(kernel, out_shape=[jax.ShapeDtypeStruct(s, F32) for s in o...  5.31 us
    all_to_all x1, starting transfers between devices, on_device(): shares = lax.all_to_all(share, 'z', 0, 0, tiled=True)  4.8 us
    pallas_call x1, Pallas kernels, on_device(): pl.pallas_call(project_deep, out_shape=[jax.ShapeDtypeStruct((rows, 128),...  3.17 us
    unnamed x6, local copies, waits for them, and re-layouts  1.9 us
  transfers between devices with their start and end apart: 14, of which 9 were waited for; matrix products, arithmetic and copies ran while one was open for 0% of the time, Pallas kernels for 0%

profile of v2, /device:TPU:32, one launch (start us, length us, event | category | flops | bytes accessed | tf_op | source)
XLA Modules:
  0.0 82.5 jit_solution(6175144836573223188)
XLA Ops:
  0.6 0.0 copy-start.2
  0.6 0.0 copy-start.1
  0.7 0.8 reshape.28.deep_ref
  1.4 0.0 copy-start
  1.4 1.9 %copy-done = f32[6,64,16,128]{3,2,1,0:T(8,128)S(1)} copy-done((f32[6,64,16,128]{3,2,1,0:T(8,128)S(1)}, f32[6,64,16,128]{3,2,1,0:T(8,128)}, u32[]{:S(2)}) %copy-start) | copy-done | bytes 3145752
  3.3 3.2 %shard_map.59 = (f32[1152,128]{1,0:T(8,128)S(1)}, f32[1152,128]{1,0:T(8,128)S(1)}) custom-call(f32[6,64,16,128]{3,2,1,0:T(8,128)S(1)} %copy-done, f32[8,6,128]{2,1,0:T(8,128)S(1)} %reshape.28.deep_ref), custom_call_target="tpu_custom_call" | custom-call | tf_op jit(solution)/shard_map/pallas_call | solution.py:169
  6.5 0.1 collective-permute-start
  6.6 2.0 %collective-permute-done = f32[1152,128]{1,0:T(8,128)S(1)} collective-permute-done((f32[1152,128]{1,0:T(8,128)S(1)}, f32[1152,128]{1,0:T(8,128)S(1)}, u32[]{:S(2)}, u32[]{:S(2)}) %collective-permute-start) | collective-permute-done | bytes 589856 | tf_op jit(solution)/shard_map/ppermute | solution.py:163
  8.6 0.1 slice_add_fusion
  8.6 2.8 %collective-permute-start.3 = (f32[288,128]{1,0:T(8,128)S(1)}, f32[288,128]{1,0:T(8,128)S(1)}, u32[]{:S(2)}, u32[]{:S(2)}) collective-permute-start(f32[288,128]{1,0:T(8,128)S(1)} %get-tuple-element.14), channel_id=1, source_target_pairs={{0,6},{2,4},{4,2},{6,0},{1,7},{3,5},{5,3},{7,1},{8,14},{10,12},{12... | collective-permute-start | bytes 442376 | tf_op jit(solution)/shard_map/ppermute | solution.py:163
  11.5 0.8 collective-permute-start.2
  12.3 0.5 collective-permute-start.1
  12.8 5.4 %collective-permute-done.3.d_ref = f32[288,128]{1,0:T(8,128)S(1)} collective-permute-done((f32[288,128]{1,0:T(8,128)S(1)}, f32[288,128]{1,0:T(8,128)S(1)}, u32[]{:S(2)}, u32[]{:S(2)}) %collective-permute-start.3) | collective-permute-done | bytes 147488 | tf_op jit(solution)/shard_map/ppermute | solution.py:163
  18.2 1.5 %collective-permute-done.2.c_ref = f32[288,128]{1,0:T(8,128)S(1)} collective-permute-done((f32[288,128]{1,0:T(8,128)S(1)}, f32[288,128]{1,0:T(8,128)S(1)}, u32[]{:S(2)}, u32[]{:S(2)}) %collective-permute-start.2) | collective-permute-done | bytes 147488 | tf_op jit(solution)/shard_map/ppermute | solution.py:163
  19.7 0.0 collective-permute-done.1.b_ref
  19.7 0.0 copy-done.2
  19.7 0.2 shard_map.60
  19.9 17.2 %all_to_all.10.got_ref = f32[8,7,8,128]{3,2,1,0:T(8,128)S(1)} all-to-all(f32[8,7,8,128]{3,2,1,0:T(8,128)S(1)} %shard_map.60), channel_id=1, replica_groups=mesh['yh'=2,'z'=8,'yl'=2,'x'=4,'core'=2] {'z'}, dimensions={0} | all-to-all | bytes 458752 | tf_op jit(solution)/shard_map/all_to_all | solution.py:182
  37.1 0.0 copy-done.1
  37.1 0.7 shard_map.61
  37.8 3.3 %collective-permute-start.5 = (f32[304,128]{1,0:T(8,128)S(1)}, f32[304,128]{1,0:T(8,128)S(1)}, u32[]{:S(2)}, u32[]{:S(2)}) collective-permute-start(f32[304,128]{1,0:T(8,128)S(1)} %get-tuple-element.11), channel_id=1, source_target_pairs={{0,128},{8,136},{128,0},{136,8},{1,129},{9,137},{129,1},{137,9},{2... | collective-permute-start | bytes 466952 | tf_op jit(solution)/shard_map/ppermute | solution.py:163
  41.1 1.1 %collective-permute-start.6 = (f32[240,128]{1,0:T(8,128)S(1)}, f32[240,128]{1,0:T(8,128)S(1)}, u32[]{:S(2)}, u32[]{:S(2)}) collective-permute-start(f32[240,128]{1,0:T(8,128)S(1)} %get-tuple-element.10.own_ref), channel_id=1, source_target_pairs={{0,136},{8,128},{128,8},{136,0},{1,137},{9,129},{129,9},{137,1},{2... | collective-permute-start | bytes 368648 | tf_op jit(solution)/shard_map/ppermute | solution.py:163
  42.1 0.0 collective-permute-start.4
  42.1 5.1 %collective-permute-done.6.r3 = f32[240,128]{1,0:T(8,128)S(1)} collective-permute-done((f32[240,128]{1,0:T(8,128)S(1)}, f32[240,128]{1,0:T(8,128)S(1)}, u32[]{:S(2)}, u32[]{:S(2)}) %collective-permute-start.6) | collective-permute-done | bytes 122912 | tf_op jit(solution)/shard_map/ppermute | solution.py:163
  47.2 0.0 collective-permute-done.4.r1
  47.2 0.0 collective-permute-done.5.r2
  47.2 1.1 %shard_map.62 = (f32[96,128]{1,0:T(8,128)S(1)}, f32[8,5,8,128]{3,2,1,0:T(8,128)}) custom-call(f32[240,128]{1,0:T(8,128)S(1)} %get-tuple-element.10.own_ref, f32[240,128]{1,0:T(8,128)S(1)} %collective-permute-done.4.r1, f32[304,128]{1,0:T(8,128)S(1)} %collective-permute-done.5.r2, f32[240,128]{1,0:T(8,128)S(1)} %collective-permute-done.6.r3, ...), custom_call_target="tpu_custom_call" | custom-call | tf_op jit(solution)/shard_map/pallas_call | solution.py:152
  48.3 0.0 collective-permute-start.7
  48.3 4.8 %all-to-all-start.1 = ((f32[8,5,8,128]{3,2,1,0:T(8,128)}), f32[8,5,8,128]{3,2,1,0:T(8,128)S(1)}, u32[]{:S(2)}, u32[]{:S(2)}) async-start(f32[8,5,8,128]{3,2,1,0:T(8,128)} %get-tuple-element.13), calls=%async_computation.1 | async-start | bytes 327680 | tf_op jit(solution)/shard_map/all_to_all | solution.py:188
  53.1 0.0 collective-permute-done.7
  53.1 1.6 %collective-permute-start.8 = (f32[96,128]{1,0:T(8,128)S(1)}, f32[96,128]{1,0:T(8,128)S(1)}, u32[]{:S(2)}, u32[]{:S(2)}) collective-permute-start(f32[96,128]{1,0:T(8,128)S(1)} %add.31), channel_id=1, source_target_pairs={{0,2},{2,0},{4,6},{6,4},{1,3},{3,1},{5,7},{7,5},{8,10},{10,8},{12,... | collective-permute-start | bytes 147464 | tf_op jit(solution)/shard_map/ppermute | solution.py:163
  54.7 2.6 %collective-permute-done.8 = f32[96,128]{1,0:T(8,128)S(1)} collective-permute-done((f32[96,128]{1,0:T(8,128)S(1)}, f32[96,128]{1,0:T(8,128)S(1)}, u32[]{:S(2)}, u32[]{:S(2)}) %collective-permute-start.8) | collective-permute-done | bytes 49184 | tf_op jit(solution)/shard_map/ppermute | solution.py:163
  57.3 2.8 %collective-permute-start.9 = (f32[96,128]{1,0:T(8,128)S(1)}, f32[96,128]{1,0:T(8,128)S(1)}, u32[]{:S(2)}, u32[]{:S(2)}) collective-permute-start(f32[96,128]{1,0:T(8,128)S(1)} %add.32), channel_id=1, source_target_pairs={{0,6},{2,4},{4,2},{6,0},{1,7},{3,5},{5,3},{7,1},{8,14},{10,12},{12... | collective-permute-start | bytes 147464 | tf_op jit(solution)/shard_map/ppermute | solution.py:163
  60.1 2.5 %collective-permute-done.9 = f32[96,128]{1,0:T(8,128)S(1)} collective-permute-done((f32[96,128]{1,0:T(8,128)S(1)}, f32[96,128]{1,0:T(8,128)S(1)}, u32[]{:S(2)}, u32[]{:S(2)}) %collective-permute-start.9) | collective-permute-done | bytes 49184 | tf_op jit(solution)/shard_map/ppermute | solution.py:163
  62.7 0.3 collective-permute-start.10
  62.9 3.9 %collective-permute-done.10 = f32[96,128]{1,0:T(8,128)S(1)} collective-permute-done((f32[96,128]{1,0:T(8,128)S(1)}, f32[96,128]{1,0:T(8,128)S(1)}, u32[]{:S(2)}, u32[]{:S(2)}) %collective-permute-start.10) | collective-permute-done | bytes 49184 | tf_op jit(solution)/shard_map/ppermute | solution.py:163
  66.9 2.5 %collective-permute-start.11 = (f32[96,128]{1,0:T(8,128)S(1)}, f32[96,128]{1,0:T(8,128)S(1)}, u32[]{:S(2)}, u32[]{:S(2)}) collective-permute-start(f32[96,128]{1,0:T(8,128)S(1)} %add.34), channel_id=1, source_target_pairs={{0,32},{16,48},{32,0},{48,16},{64,96},{80,112},{96,64},{112,80},{1... | collective-permute-start | bytes 147464 | tf_op jit(solution)/shard_map/ppermute | solution.py:163
  69.3 2.6 %collective-permute-done.11 = f32[96,128]{1,0:T(8,128)S(1)} collective-permute-done((f32[96,128]{1,0:T(8,128)S(1)}, f32[96,128]{1,0:T(8,128)S(1)}, u32[]{:S(2)}, u32[]{:S(2)}) %collective-permute-start.11) | collective-permute-done | bytes 49184 | tf_op jit(solution)/shard_map/ppermute | solution.py:163
  71.9 3.7 %collective-permute-start.12 = (f32[96,128]{1,0:T(8,128)S(1)}, f32[96,128]{1,0:T(8,128)S(1)}, u32[]{:S(2)}, u32[]{:S(2)}) collective-permute-start(f32[96,128]{1,0:T(8,128)S(1)} %add.35.p_ref), channel_id=1, source_target_pairs={{0,112},{16,96},{32,80},{48,64},{64,48},{80,32},{96,16},{112,0},{1... | collective-permute-start | bytes 147464 | tf_op jit(solution)/shard_map/ppermute | solution.py:163
  75.6 0.0 all-to-all-done.1
  75.6 3.5 %collective-permute-done.12.q_ref = f32[96,128]{1,0:T(8,128)S(1)} collective-permute-done((f32[96,128]{1,0:T(8,128)S(1)}, f32[96,128]{1,0:T(8,128)S(1)}, u32[]{:S(2)}, u32[]{:S(2)}) %collective-permute-start.12) | collective-permute-done | bytes 49184 | tf_op jit(solution)/shard_map/ppermute | solution.py:163
  79.1 3.3 %shard_map.63 = (f32[64,96]{1,0:T(8,128)}, f32[6,6,6,96]{3,2,1,0:T(8,128)}) custom-call(f32[96,128]{1,0:T(8,128)S(1)} %add.35.p_ref, f32[96,128]{1,0:T(8,128)S(1)} %collective-permute-done.12.q_ref, f32[320,128]{1,0:T(8,128)S(1)} %bitcast.2), custom_call_target="tpu_custom_call" | custom-call | tf_op jit(solution)/shard_map/pallas_call | solution.py:152
  (5 shorter events, 0.0 us)
Async XLA Ops:
  0.6 19.1 %copy-start.2 = (f32[16,96]{1,0:T(8,128)S(1)}, f32[16,96]{1,0:T(8,128)}, u32[]{:S(2)}) copy-start(f32[16,96]{1,0:T(8,128)} %mid_ref.1) | copy-start | bytes 18436
  0.6 36.5 %copy-start.1 = (f32[64,96]{1,0:T(8,128)S(1)}, f32[64,96]{1,0:T(8,128)}, u32[]{:S(2)}) copy-start(f32[64,96]{1,0:T(8,128)} %old_ref.3) | copy-start | bytes 73732
  1.4 1.9 %copy-start = (f32[6,64,16,128]{3,2,1,0:T(8,128)S(1)}, f32[6,64,16,128]{3,2,1,0:T(8,128)}, u32[]{:S(2)}) copy-start(f32[6,64,16,128]{3,2,1,0:T(8,128)} %vel_ref.1) | copy-start | bytes 9437188
  6.5 2.1 %collective-permute-start = (f32[1152,128]{1,0:T(8,128)S(1)}, f32[1152,128]{1,0:T(8,128)S(1)}, u32[]{:S(2)}, u32[]{:S(2)}) collective-permute-start(f32[1152,128]{1,0:T(8,128)S(1)} %get-tuple-element.9), channel_id=1, source_target_pairs={{0,1},{1,0},{2,3},{3,2},{4,5},{5,4},{6,7},{7,6},{8,9},{9,8},{10,11... | collective-permute-start | bytes 1769480 | tf_op jit(solution)/shard_map/ppermute | solution.py:163
  8.6 9.6 %collective-permute-start.3 = (f32[288,128]{1,0:T(8,128)S(1)}, f32[288,128]{1,0:T(8,128)S(1)}, u32[]{:S(2)}, u32[]{:S(2)}) collective-permute-start(f32[288,128]{1,0:T(8,128)S(1)} %get-tuple-element.14), channel_id=1, source_target_pairs={{0,6},{2,4},{4,2},{6,0},{1,7},{3,5},{5,3},{7,1},{8,14},{10,12},{12... | collective-permute-start | bytes 442376 | tf_op jit(solution)/shard_map/ppermute | solution.py:163
  11.5 8.2 %collective-permute-start.2 = (f32[288,128]{1,0:T(8,128)S(1)}, f32[288,128]{1,0:T(8,128)S(1)}, u32[]{:S(2)}, u32[]{:S(2)}) collective-permute-start(f32[288,128]{1,0:T(8,128)S(1)} %get-tuple-element.15), channel_id=1, source_target_pairs={{0,4},{2,6},{4,0},{6,2},{1,5},{3,7},{5,1},{7,3},{8,12},{10,14},{12... | collective-permute-start | bytes 442376 | tf_op jit(solution)/shard_map/ppermute | solution.py:163
  12.3 7.4 %collective-permute-start.1 = (f32[288,128]{1,0:T(8,128)S(1)}, f32[288,128]{1,0:T(8,128)S(1)}, u32[]{:S(2)}, u32[]{:S(2)}) collective-permute-start(f32[288,128]{1,0:T(8,128)S(1)} %get-tuple-element.16), channel_id=1, source_target_pairs={{0,2},{2,0},{4,6},{6,4},{1,3},{3,1},{5,7},{7,5},{8,10},{10,8},{12,... | collective-permute-start | bytes 442376 | tf_op jit(solution)/shard_map/ppermute | solution.py:163
  37.8 9.4 %collective-permute-start.5 = (f32[304,128]{1,0:T(8,128)S(1)}, f32[304,128]{1,0:T(8,128)S(1)}, u32[]{:S(2)}, u32[]{:S(2)}) collective-permute-start(f32[304,128]{1,0:T(8,128)S(1)} %get-tuple-element.11), channel_id=1, source_target_pairs={{0,128},{8,136},{128,0},{136,8},{1,129},{9,137},{129,1},{137,9},{2... | collective-permute-start | bytes 466952 | tf_op jit(solution)/shard_map/ppermute | solution.py:163
  41.1 6.1 %collective-permute-start.6 = (f32[240,128]{1,0:T(8,128)S(1)}, f32[240,128]{1,0:T(8,128)S(1)}, u32[]{:S(2)}, u32[]{:S(2)}) collective-permute-start(f32[240,128]{1,0:T(8,128)S(1)} %get-tuple-element.10.own_ref), channel_id=1, source_target_pairs={{0,136},{8,128},{128,8},{136,0},{1,137},{9,129},{129,9},{137,1},{2... | collective-permute-start | bytes 368648 | tf_op jit(solution)/shard_map/ppermute | solution.py:163
  42.1 5.1 %collective-permute-start.4 = (f32[240,128]{1,0:T(8,128)S(1)}, f32[240,128]{1,0:T(8,128)S(1)}, u32[]{:S(2)}, u32[]{:S(2)}) collective-permute-start(f32[240,128]{1,0:T(8,128)S(1)} %get-tuple-element.10.own_ref), channel_id=1, source_target_pairs={{0,8},{8,0},{128,136},{136,128},{1,9},{9,1},{129,137},{137,129},{2... | collective-permute-start | bytes 368648 | tf_op jit(solution)/shard_map/ppermute | solution.py:163
  48.3 4.8 %collective-permute-start.7 = (f32[96,128]{1,0:T(8,128)S(1)}, f32[96,128]{1,0:T(8,128)S(1)}, u32[]{:S(2)}, u32[]{:S(2)}) collective-permute-start(f32[96,128]{1,0:T(8,128)S(1)} %get-tuple-element.12), channel_id=1, source_target_pairs={{0,1},{1,0},{2,3},{3,2},{4,5},{5,4},{6,7},{7,6},{8,9},{9,8},{10,11... | collective-permute-start | bytes 147464 | tf_op jit(solution)/shard_map/ppermute | solution.py:163
  48.3 27.3 %all-to-all-start.1 = ((f32[8,5,8,128]{3,2,1,0:T(8,128)}), f32[8,5,8,128]{3,2,1,0:T(8,128)S(1)}, u32[]{:S(2)}, u32[]{:S(2)}) async-start(f32[8,5,8,128]{3,2,1,0:T(8,128)} %get-tuple-element.13), calls=%async_computation.1 | async-start | bytes 327680 | tf_op jit(solution)/shard_map/all_to_all | solution.py:188
  53.1 4.2 %collective-permute-start.8 = (f32[96,128]{1,0:T(8,128)S(1)}, f32[96,128]{1,0:T(8,128)S(1)}, u32[]{:S(2)}, u32[]{:S(2)}) collective-permute-start(f32[96,128]{1,0:T(8,128)S(1)} %add.31), channel_id=1, source_target_pairs={{0,2},{2,0},{4,6},{6,4},{1,3},{3,1},{5,7},{7,5},{8,10},{10,8},{12,... | collective-permute-start | bytes 147464 | tf_op jit(solution)/shard_map/ppermute | solution.py:163
  57.3 5.4 %collective-permute-start.9 = (f32[96,128]{1,0:T(8,128)S(1)}, f32[96,128]{1,0:T(8,128)S(1)}, u32[]{:S(2)}, u32[]{:S(2)}) collective-permute-start(f32[96,128]{1,0:T(8,128)S(1)} %add.32), channel_id=1, source_target_pairs={{0,6},{2,4},{4,2},{6,0},{1,7},{3,5},{5,3},{7,1},{8,14},{10,12},{12... | collective-permute-start | bytes 147464 | tf_op jit(solution)/shard_map/ppermute | solution.py:163
  62.7 4.2 %collective-permute-start.10 = (f32[96,128]{1,0:T(8,128)S(1)}, f32[96,128]{1,0:T(8,128)S(1)}, u32[]{:S(2)}, u32[]{:S(2)}) collective-permute-start(f32[96,128]{1,0:T(8,128)S(1)} %add.33), channel_id=1, source_target_pairs={{0,16},{16,0},{32,48},{48,32},{64,80},{80,64},{96,112},{112,96},{1... | collective-permute-start | bytes 147464 | tf_op jit(solution)/shard_map/ppermute | solution.py:163
  66.9 5.1 %collective-permute-start.11 = (f32[96,128]{1,0:T(8,128)S(1)}, f32[96,128]{1,0:T(8,128)S(1)}, u32[]{:S(2)}, u32[]{:S(2)}) collective-permute-start(f32[96,128]{1,0:T(8,128)S(1)} %add.34), channel_id=1, source_target_pairs={{0,32},{16,48},{32,0},{48,16},{64,96},{80,112},{96,64},{112,80},{1... | collective-permute-start | bytes 147464 | tf_op jit(solution)/shard_map/ppermute | solution.py:163
  71.9 7.2 %collective-permute-start.12 = (f32[96,128]{1,0:T(8,128)S(1)}, f32[96,128]{1,0:T(8,128)S(1)}, u32[]{:S(2)}, u32[]{:S(2)}) collective-permute-start(f32[96,128]{1,0:T(8,128)S(1)} %add.35.p_ref), channel_id=1, source_target_pairs={{0,112},{16,96},{32,80},{48,64},{64,48},{80,32},{96,16},{112,0},{1... | collective-permute-start | bytes 147464 | tf_op jit(solution)/shard_map/ppermute | solution.py:163

commit v3 on v2

--- a/solution.py
+++ b/solution.py
@@ -9,9 +9,11 @@
 F32, BF16 = jnp.float32, jnp.bfloat16
 K, R1, NX = 6, 96, 128
 XS, CORES, ZS, YS = 4, 2, 8, 4
+KP, PP = 3, 18
 PAIRS = 36
 SLOTS = 5
 TILES = 7
+G1, G2, G3 = 1, 2, 7
 HALF = SLOTS * 48
 
 
@@ -24,27 +26,43 @@
     return high, (value - high.astype(F32)).astype(BF16)
 
 
-def project_deep(vel_ref, deep_ref, send_ref, keep_ref, cells_ref, sems):
-    copies = [pltpu.make_async_copy(vel_ref.at[k], cells_ref.at[k], sems.at[k]) for k in range(K)]
+def project_cells(k, cells_ref, deep, send_ref, keep_ref):
+    for i in range(0, 8, 2):
+        cells = jnp.concatenate([cells_ref[k, :, b, :] for b in range(2 * i, 2 * i + 4)], axis=0)
+        out = dot(deep, jnp.concatenate(halves(cells), axis=1), 1, 1, None)
+        out = out[:48] + out[48:]
+        for s in range(2):
+            at = pl.ds(k * 8 + i + s, 24, stride=KP * 8)
+            send_ref[at, :] = out[:24, s * 128:s * 128 + 128]
+            keep_ref[at, :] = out[24:, s * 128:s * 128 + 128]
+
+
+def ranks(deep_ref):
+    me = lax.axis_index("x") * CORES + lax.axis_index("core")
+    rows = [deep_ref[pl.ds((me ^ (x * CORES + core)) * 6, 6), :] for core in (1, 0) for x in range(XS)]
+    high, low = halves(jnp.concatenate(rows, axis=0))
+    return jnp.concatenate([jnp.concatenate([high, high], axis=1), jnp.concatenate([low, low], axis=1)], axis=0)
+
+
+def project_first(vel_ref, deep_ref, send_ref, keep_ref, next_ref, cells_ref, sems):
+    copies = [pltpu.make_async_copy(vel_ref.at[k], cells_ref.at[k], sems.at[k]) for k in range(KP)]
+    copies.append(pltpu.make_async_copy(vel_ref.at[pl.ds(KP, K - KP)], next_ref, sems.at[KP]))
     for copy in copies:
         copy.start()
-    me = lax.axis_index("x") * CORES + lax.axis_index("core")
-    rows = [deep_ref[me ^ (x * CORES + core)] for core in (1, 0) for x in range(XS)]
-    high, low = halves(jnp.concatenate(rows, axis=0))
-    deep = jnp.concatenate([jnp.concatenate([high, high], axis=1), jnp.concatenate([low, low], axis=1)], axis=0)
-    for k in range(K):
+    deep = ranks(deep_ref)
+    for k in range(KP):
         copies[k].wait()
-        for i in range(0, 8, 2):
-            cells = jnp.concatenate([cells_ref[k, :, b, :] for b in range(2 * i, 2 * i + 4)], axis=0)
-            part = dot(deep, jnp.concatenate(halves(cells), axis=1), 1, 1, None)
-            part = part[:48] + part[48:]
-            for s in range(2):
-                at = pl.ds(k * 8 + i + s, 24, stride=48)
-                send_ref[at, :] = part[:24, s * 128:s * 128 + 128]
-                keep_ref[at, :] = part[24:, s * 128:s * 128 + 128]
-
-
-def pack_depth(a_ref, b_ref, c_ref, d_ref, mid_ref, out_ref):
+        project_cells(k, cells_ref, deep, send_ref, keep_ref)
+    copies[KP].wait()
+
+
+def project_rest(cells_ref, deep_ref, send_ref, keep_ref):
+    deep = ranks(deep_ref)
+    for k in range(KP):
+        project_cells(k, cells_ref, deep, send_ref, keep_ref)
+
+
+def pack_depth(a0, b0, c0, d0, a1, b1, c1, d1, mid_ref, out_ref):
     source = lax.broadcasted_iota(jnp.int32, (R1, 128), 0)
     lane = lax.broadcasted_iota(jnp.int32, (R1, 128), 1)
     yl = jnp.where(lane >= 48, 1, 0)
@@ -57,8 +75,9 @@
         for slot in range(SLOTS):
             pair = dest * SLOTS + slot
             if pair < PAIRS:
-                at = pl.ds(pair * 8, 8)
-                out_ref[dest, slot] = (a_ref[at, :] + b_ref[at, :]) + (c_ref[at, :] + d_ref[at, :])
+                a, b, c, d = (a0, b0, c0, d0) if pair < PP else (a1, b1, c1, d1)
+                at = pl.ds(pair % PP * 8, 8)
+                out_ref[dest, slot] = (a[at, :] + b[at, :]) + (c[at, :] + d[at, :])
             else:
                 out_ref[dest, slot] = jnp.zeros((8, 128), F32)
         out_ref[dest, 5] = even
@@ -81,8 +100,8 @@
     more_ref[HALF:HALF + 64, :] = jnp.concatenate([old_ref[...], jnp.zeros((64, 128 - R1), F32)], axis=1)
 
 
-def form_image(own_ref, r1, r2, r3, old_ref, image_ref, share_ref):
-    yh, yl = lax.axis_index("yh"), lax.axis_index("yl")
+def form_image(own_ref, r1, r2, r3, old_ref, image_ref, a1_ref, a2_ref, a3_ref, a0_ref, mine_ref):
+    yh, yl, z = lax.axis_index("yh"), lax.axis_index("yl"), lax.axis_index("z")
     near = own_ref[...] + r1[...]
     far = r2[:HALF, :] + r3[...]
     h0 = jnp.where(yh == 0, near, far)
@@ -90,16 +109,23 @@
     low = lax.broadcasted_iota(jnp.int32, (HALF, 128), 1) < 64
     p0 = jnp.where(low, h0, pltpu.roll(h1, 64, 1))
     p1 = jnp.where(low, pltpu.roll(h0, 64, 1), h1)
-    mine = jnp.where(yl == 0, p0, p1)
-    for slot in range(SLOTS):
-        for z in range(ZS):
-            share_ref[z, slot, 0:6, :] = mine[slot * 48 + z * 6:slot * 48 + z * 6 + 6]
     stack = jnp.concatenate([p0, p1], axis=0)
     square = dot(stack, stack, 0, 0)
     other = r2[HALF:HALF + 64, :R1]
     own = old_ref[...]
     old = jnp.concatenate([jnp.where(yh == 0, own, other), jnp.where(yh == 0, other, own)], axis=0)
     image_ref[...] = dot(old, square, 0, 0)
+    mine_ref[...] = jnp.where(yl == 0, p0, p1)
+    plan = (
+        (a1_ref, (G1 ^ G2, G1 ^ G2 ^ G3, G1 ^ G3, G1)),
+        (a2_ref, (G2, G2 ^ G3)),
+        (a3_ref, (G3,)),
+        (a0_ref, (0,)),
+    )
+    for ref, places in plan:
+        for i, m in enumerate(places):
+            for slot in range(SLOTS):
+                ref[i, slot, 0:6, :] = mine_ref[pl.ds(slot * 48 + (z ^ m) * 6, 6), :]
 
 
 def solve(gram, image_t):
@@ -131,16 +157,19 @@
     return jnp.concatenate(done, axis=0)
 
 
-def finish(p_ref, q_ref, share_ref, basis_ref, core_ref, rows_ref, turn_ref):
+def finish(p_ref, q_ref, a0_ref, r1_ref, r2_ref, r3_ref, basis_ref, core_ref, rows_ref, turn_ref):
+    yh, z = lax.axis_index("yh"), lax.axis_index("z")
+    held = [(0, a0_ref, 0), (G1, r1_ref, 3), (G2, r2_ref, 0), (G1 ^ G2, r2_ref, 2)]
+    held += [(G3 ^ m, r3_ref, i) for i, m in enumerate((0, G1, G2, G1 ^ G2))]
+    for m, ref, i in held:
+        for slot in range(SLOTS):
+            pair = (z ^ m) * SLOTS + slot
+            at = jnp.where(pair < PAIRS, pair % PP // KP * 8 + pair // PP * KP + pair % KP, 7)
+            rows_ref[pl.ds(at, 6, stride=48), :] = ref[i, slot, 0:6, :]
     image_t = p_ref[...] + q_ref[...]
     basis_t = solve(dot(image_t, image_t, 1, 1), image_t)
     turn_ref[...] = basis_t.T
-    yh = lax.axis_index("yh")
     basis_ref[...] = turn_ref[pl.ds(pl.multiple_of(yh * 64, 64), 64), :]
-    for t in range(6):
-        for r in range(6):
-            rows_ref[pl.ds((t * 6 + r) * 8, 6), :] = share_ref[pl.ds(r * 48 + t, 6, stride=8), :]
-            rows_ref[pl.ds((t * 6 + r) * 8 + 6, 2), :] = jnp.zeros((2, 128), F32)
     core = dot(rows_ref[...], basis_t, 1, 1)
     core_ref[...] = core.reshape(6, 6, 8, R1)[:, :, :6, :]
 
@@ -163,36 +192,60 @@
     return lax.ppermute(value, axis, [(i, i ^ bit) for i in range(size)])
 
 
+def across(value, a, b):
+    axes = ("z", "x", "core")
+    one, two, both = (
+        lax.ppermute(value, axes, [(i, i ^ m) for i in range(ZS * XS * CORES)]) for m in (a, b, a ^ b)
+    )
+    return (value + one) + (two + both)
+
+
+def shift(value, by):
+    return lax.ppermute(value, "z", [(i, (i - by) % ZS) for i in range(ZS)])
+
+
 def on_device(velocity, basis_old, basis_mid, basis_deep):
-    deep = basis_deep.T.reshape(8, 6, 128)
-    rows = XS * PAIRS * 8
-    send, keep = pl.pallas_call(
-        project_deep,
-        out_shape=[jax.ShapeDtypeStruct((rows, 128), F32)] * 2,
+    deep = basis_deep.T
+    parts = [(XS * PP * 8, 128)] * 2
+    send, keep, cells = pl.pallas_call(
+        project_first,
+        out_shape=[jax.ShapeDtypeStruct(s, F32) for s in (*parts, (K - KP, 64, 16, 128))],
         in_specs=[pl.BlockSpec(memory_space=pltpu.HBM), VMEM],
-        out_specs=[VMEM] * 2,
-        scratch_shapes=[pltpu.VMEM((K, 64, 16, 128), F32), pltpu.SemaphoreType.DMA((K,))],
-        compiler_params=pltpu.CompilerParams(vmem_limit_bytes=32 * 2**20),
+        out_specs=[VMEM] * 3,
+        scratch_shapes=[pltpu.VMEM((KP, 64, 16, 128), F32), pltpu.SemaphoreType.DMA((KP + 1,))],
+        compiler_params=pltpu.CompilerParams(vmem_limit_bytes=51 * 2**20),
     )(velocity, deep)
-    got = swap(send, "core", CORES, 1)
-    keep, got = (v.reshape(XS, PAIRS * 8, 128) for v in (keep, got))
-    sums = [keep[m] + got[m] for m in range(XS)]
-    others = {m: swap(sums[m], "x", XS, m) for m in (3, 1, 2)}
-    (packed,) = call(pack_depth, [(ZS, TILES, 8, 128)], sums[0], others[1], others[2], others[3], basis_mid)
+    sums = []
+    for part in range(2):
+        if part:
+            send, keep = call(project_rest, parts, cells, deep)
+        got = swap(send, "core", CORES, 1)
+        keep, got = (v.reshape(XS, PP * 8, 128) for v in (keep, got))
+        own = [keep[m] + got[m] for m in range(XS)]
+        others = {m: swap(own[m], "x", XS, m) for m in (3, 1, 2)}
+        sums += [own[0], others[1], others[2], others[3]]
+    (packed,) = call(pack_depth, [(ZS, TILES, 8, 128)], *sums, basis_mid)
     mine = lax.all_to_all(packed, "z", 0, 0, tiled=True)
     part, more = call(project_mid, [(HALF, 128), (HALF + 64, 128)], mine, basis_old)
     near = {m: swap(more if m == 2 else part, ("yh", "yl"), YS, m) for m in (3, 1, 2)}
-    image, share = call(
-        form_image, [(R1, NX), (ZS, SLOTS, 8, 128)], part, near[1], near[2], near[3], basis_old
-    )
-    shares = lax.all_to_all(share, "z", 0, 0, tiled=True)
-    for axis, size, bit in (("core", 2, 1), ("x", 4, 1), ("x", 4, 3), ("z", 8, 1), ("z", 8, 2)):
-        image = image + swap(image, axis, size, bit)
-    last = swap(image, "z", 8, 7)
+    block = (SLOTS, 8, 128)
+    image, a1, a2, a3, a0 = call(
+        form_image,
+        [(R1, NX), (4, *block), (2, *block), (1, *block), (1, *block)],
+        part, near[1], near[2], near[3], basis_old,
+        scratch=[(HALF, 128)],
+    )
+    b1 = swap(a1, "z", ZS, G1)
+    b2 = swap(jnp.concatenate([a2, b1[:2]]), "z", ZS, G2)
+    b3 = swap(jnp.concatenate([a3, b1[2:3], b2[1:2], b2[3:4]]), "z", ZS, G3)
+    image = across(image, 1, 2)
+    image = across(image, 6, 8)
+    image = image + swap(image, "z", 8, 2)
+    last = swap(image, "z", ZS, 7)
     basis_new, core_block = call(
         finish,
         [(64, R1), (6, 6, 6, R1)],
-        image, last, shares.reshape(ZS * SLOTS * 8, 128),
+        image, last, a0, b1, b2, b3,
         scratch=[(288, 128), (NX, R1)],
     )
     return (basis_new, core_block)

time: 82.8 us -> 75.9 us (0.917)
  waiting for transfers between devices: 29.1 us -> 21 us
  starting transfers between devices: 24.2 us -> 27.5 us
  local copies, waits for them, and re-layouts: 2.65 us -> 0.75 us
    ppermute x13 -> x16, waiting for transfers between devices: 29.1 us -> 17.4 us  [swap(): return lax.ppermute(value, axis, [(i, i ^ bit) for i in range(size)])]
    ppermute x0 -> x6, starting transfers between devices: none -> 6.91 us  [across(): lax.ppermute(value, axes, [(i, i ^ m) for i in range(ZS * XS * CORES)])]
    all_to_all x1 -> x0, starting transfers between devices: 4.8 us -> none  [on_device(): shares = lax.all_to_all(share, 'z', 0, 0, tiled=True)]
    ppermute x0 -> x6, waiting for transfers between devices: none -> 3.64 us  [across(): lax.ppermute(value, axes, [(i, i ^ m) for i in range(ZS * XS * CORES)])]
    unnamed x6, local copies, waits for them, and re-layouts: 1.9 us -> 0.74 us
    ppermute x13 -> x16, starting transfers between devices: 19.4 us -> 20.6 us  [swap(): return lax.ppermute(value, axis, [(i, i ^ bit) for i in range(size)])]
    pallas_call x4 -> x5, Pallas kernels: 5.31 us -> 6.35 us  [call(): pl.pallas_call(kernel, out_shape=[jax.ShapeDtypeStruct(s, F32) for s in o...]
  transfers between devices with their start and end apart: 14 -> 22, of which waited for: 9 -> 11; matrix products, arithmetic and copies ran while one was open for 0% -> 0% of each run, Pallas kernels for 0% -> 1%
where the time goes in v3:
time: 75.9 us; the launch traced here: 75.7 us
  starting transfers between devices  27.5 us (36%)
  waiting for transfers between devices  21 us (28%)
  blocking collectives  16.8 us (22%)
  Pallas kernels  8.84 us (12%)
    ppermute x16, starting transfers between devices, swap(): return lax.ppermute(value, axis, [(i, i ^ bit) for i in range(size)])  20.6 us
    ppermute x16, waiting for transfers between devices, swap(): return lax.ppermute(value, axis, [(i, i ^ bit) for i in range(size)])  17.4 us
    all_to_all x1, blocking collectives, on_device(): mine = lax.all_to_all(packed, 'z', 0, 0, tiled=True)  16.8 us
    ppermute x6, starting transfers between devices, across(): lax.ppermute(value, axes, [(i, i ^ m) for i in range(ZS * XS * CORES)])  6.91 us
    pallas_call x5, Pallas kernels, call(): pl.pallas_call(kernel, out_shape=[jax.ShapeDtypeStruct(s, F32) for s in o...  6.35 us
    ppermute x6, waiting for transfers between devices, across(): lax.ppermute(value, axes, [(i, i ^ m) for i in range(ZS * XS * CORES)])  3.64 us
    pallas_call x1, Pallas kernels, on_device(): pl.pallas_call(project_first, out_shape=[jax.ShapeDtypeStruct(s, F32) for...  2.48 us
  transfers between devices with their start and end apart: 22, of which 11 were waited for; matrix products, arithmetic and copies ran while one was open for 0% of the time, Pallas kernels for 1%

profile of v3, /device:TPU:32, one launch (start us, length us, event | category | flops | bytes accessed | tf_op | source)
XLA Modules:
  0.0 75.7 jit_solution(4811910689484921792)
XLA Ops:
  0.6 0.7 copy-done.1
  1.4 2.5 %shard_map.59 = (f32[576,128]{1,0:T(8,128)S(1)}, f32[576,128]{1,0:T(8,128)S(1)}, f32[3,64,16,128]{3,2,1,0:T(8,128)S(1)}) custom-call(f32[6,64,16,128]{3,2,1,0:T(8,128)} %vel_ref.1, f32[48,128]{1,0:T(8,128)S(1)} %bitcast.1), custom_call_target="tpu_custom_call" | custom-call | tf_op jit(solution)/shard_map/pallas_call | solution.py:210
  3.9 0.1 collective-permute-start
  4.0 1.1 %shard_map.60 = (f32[576,128]{1,0:T(8,128)S(1)}, f32[576,128]{1,0:T(8,128)S(1)}) custom-call(f32[3,64,16,128]{3,2,1,0:T(8,128)S(1)} %get-tuple-element.16.cells_ref, f32[48,128]{1,0:T(8,128)S(1)} %bitcast.2), custom_call_target="tpu_custom_call" | custom-call | tf_op jit(solution)/shard_map/pallas_call | solution.py:181
  5.1 0.6 collective-permute-start.4
  5.7 0.0 collective-permute-done
  5.7 2.8 %collective-permute-start.3 = (f32[144,128]{1,0:T(8,128)S(1)}, f32[144,128]{1,0:T(8,128)S(1)}, u32[]{:S(2)}, u32[]{:S(2)}) collective-permute-start(f32[144,128]{1,0:T(8,128)S(1)} %get-tuple-element.30), channel_id=1, source_target_pairs={{0,6},{2,4},{4,2},{6,0},{1,7},{3,5},{5,3},{7,1},{8,14},{10,12},{12... | collective-permute-start | bytes 221192 | tf_op jit(solution)/shard_map/ppermute | solution.py:192
  8.6 0.8 %collective-permute-start.2 = (f32[144,128]{1,0:T(8,128)S(1)}, f32[144,128]{1,0:T(8,128)S(1)}, u32[]{:S(2)}, u32[]{:S(2)}) collective-permute-start(f32[144,128]{1,0:T(8,128)S(1)} %get-tuple-element.31), channel_id=1, source_target_pairs={{0,4},{2,6},{4,0},{6,2},{1,5},{3,7},{5,1},{7,3},{8,12},{10,14},{12... | collective-permute-start | bytes 221192 | tf_op jit(solution)/shard_map/ppermute | solution.py:192
  9.4 0.5 collective-permute-start.1
  9.9 0.0 collective-permute-done.4
  9.9 2.8 %collective-permute-start.7 = (f32[144,128]{1,0:T(8,128)S(1)}, f32[144,128]{1,0:T(8,128)S(1)}, u32[]{:S(2)}, u32[]{:S(2)}) collective-permute-start(f32[144,128]{1,0:T(8,128)S(1)} %get-tuple-element.26), channel_id=1, source_target_pairs={{0,6},{2,4},{4,2},{6,0},{1,7},{3,5},{5,3},{7,1},{8,14},{10,12},{12... | collective-permute-start | bytes 221192 | tf_op jit(solution)/shard_map/ppermute | solution.py:192
  12.8 0.8 %collective-permute-start.6 = (f32[144,128]{1,0:T(8,128)S(1)}, f32[144,128]{1,0:T(8,128)S(1)}, u32[]{:S(2)}, u32[]{:S(2)}) collective-permute-start(f32[144,128]{1,0:T(8,128)S(1)} %get-tuple-element.27), channel_id=1, source_target_pairs={{0,4},{2,6},{4,0},{6,2},{1,5},{3,7},{5,1},{7,3},{8,12},{10,14},{12... | collective-permute-start | bytes 221192 | tf_op jit(solution)/shard_map/ppermute | solution.py:192
  13.6 0.0 collective-permute-done.3.d0
  13.6 0.5 collective-permute-start.5
  14.1 0.7 collective-permute-done.2.c0
  14.8 0.0 collective-permute-done.1.b0
  14.8 0.8 %collective-permute-done.7.d1 = f32[144,128]{1,0:T(8,128)S(1)} collective-permute-done((f32[144,128]{1,0:T(8,128)S(1)}, f32[144,128]{1,0:T(8,128)S(1)}, u32[]{:S(2)}, u32[]{:S(2)}) %collective-permute-start.7) | collective-permute-done | bytes 73760 | tf_op jit(solution)/shard_map/ppermute | solution.py:192
  15.6 3.1 %collective-permute-done.6.c1 = f32[144,128]{1,0:T(8,128)S(1)} collective-permute-done((f32[144,128]{1,0:T(8,128)S(1)}, f32[144,128]{1,0:T(8,128)S(1)}, u32[]{:S(2)}, u32[]{:S(2)}) %collective-permute-start.6) | collective-permute-done | bytes 73760 | tf_op jit(solution)/shard_map/ppermute | solution.py:192
  18.6 0.0 collective-permute-done.5.b1
  18.7 0.2 shard_map.61
  18.9 16.8 %all_to_all.5.got_ref = f32[8,7,8,128]{3,2,1,0:T(8,128)S(1)} all-to-all(f32[8,7,8,128]{3,2,1,0:T(8,128)S(1)} %shard_map.61), channel_id=1, replica_groups=mesh['yh'=2,'z'=8,'yl'=2,'x'=4,'core'=2] {'z'}, dimensions={0} | all-to-all | bytes 458752 | tf_op jit(solution)/shard_map/all_to_all | solution.py:228
  35.7 0.7 shard_map.62
  36.3 3.3 %collective-permute-start.9 = (f32[304,128]{1,0:T(8,128)S(1)}, f32[304,128]{1,0:T(8,128)S(1)}, u32[]{:S(2)}, u32[]{:S(2)}) collective-permute-start(f32[304,128]{1,0:T(8,128)S(1)} %get-tuple-element.20), channel_id=1, source_target_pairs={{0,128},{8,136},{128,0},{136,8},{1,129},{9,137},{129,1},{137,9},{2... | collective-permute-start | bytes 466952 | tf_op jit(solution)/shard_map/ppermute | solution.py:192
  39.6 1.1 %collective-permute-start.10 = (f32[240,128]{1,0:T(8,128)S(1)}, f32[240,128]{1,0:T(8,128)S(1)}, u32[]{:S(2)}, u32[]{:S(2)}) collective-permute-start(f32[240,128]{1,0:T(8,128)S(1)} %get-tuple-element.19.own_ref), channel_id=1, source_target_pairs={{0,136},{8,128},{128,8},{136,0},{1,137},{9,129},{129,9},{137,1},{2... | collective-permute-start | bytes 368648 | tf_op jit(solution)/shard_map/ppermute | solution.py:192
  40.7 5.0 %collective-permute-done.10.r3 = f32[240,128]{1,0:T(8,128)S(1)} collective-permute-done((f32[240,128]{1,0:T(8,128)S(1)}, f32[240,128]{1,0:T(8,128)S(1)}, u32[]{:S(2)}, u32[]{:S(2)}) %collective-permute-start.10) | collective-permute-done | bytes 122912 | tf_op jit(solution)/shard_map/ppermute | solution.py:192
  45.7 0.8 %shard_map.63 = (f32[96,128]{1,0:T(8,128)S(1)}, f32[4,5,8,128]{3,2,1,0:T(8,128)S(1)}, f32[2,5,8,128]{3,2,1,0:T(8,128)S(1)}, f32[1,5,8,128]{3,2,1,0:T(8,128)S(1)}, f32[1,5,8,128]{3,2,1,0:T(8,128)S(1)}) custom-call(f32[240,128]{1,0:T(8,128)S(1)} %get-tuple-element.19.own_ref, f32[240,128]{1,0:T(8,128)S(1)} %collective-permute-done.8.r1, ...), custom_call_target="tpu_custom_call" | custom-call | tf_op jit(solution)/shard_map/pallas_call | solution.py:181
  46.5 0.1 collective-permute-start.13
  46.6 0.3 collective-permute-start.12
  46.9 1.5 %collective-permute-start.11 = (f32[96,128]{1,0:T(8,128)S(1)}, f32[96,128]{1,0:T(8,128)S(1)}, u32[]{:S(2)}, u32[]{:S(2)}) collective-permute-start(f32[96,128]{1,0:T(8,128)S(1)} %get-tuple-element.21), channel_id=1, source_target_pairs={{0,1},{1,0},{2,3},{3,2},{4,5},{5,4},{6,7},{7,6},{16,17},{17,16},{1... | collective-permute-start | bytes 147464 | tf_op jit(solution)/shard_map/ppermute | solution.py:198
  48.5 1.7 %collective-permute-start.19 = (f32[4,5,8,128]{3,2,1,0:T(8,128)S(1)}, f32[4,5,8,128]{3,2,1,0:T(8,128)S(1)}, u32[]{:S(2)}, u32[]{:S(2)}) collective-permute-start(f32[4,5,8,128]{3,2,1,0:T(8,128)S(1)} %get-tuple-element.23), channel_id=1, source_target_pairs={{0,16},{16,0},{32,48},{48,32},{64,80},{80,64},{96,112},{112,96},{1... | collective-permute-start | bytes 245768 | tf_op jit(solution)/shard_map/ppermute | solution.py:192
  50.2 0.0 collective-permute-done.13
  50.2 1.0 %collective-permute-done.12 = f32[96,128]{1,0:T(8,128)S(1)} collective-permute-done((f32[96,128]{1,0:T(8,128)S(1)}, f32[96,128]{1,0:T(8,128)S(1)}, u32[]{:S(2)}, u32[]{:S(2)}) %collective-permute-start.12) | collective-permute-done | bytes 49184 | tf_op jit(solution)/shard_map/ppermute | solution.py:198
  51.2 0.0 collective-permute-done.11
  51.2 2.9 %collective-permute-start.16 = (f32[96,128]{1,0:T(8,128)S(1)}, f32[96,128]{1,0:T(8,128)S(1)}, u32[]{:S(2)}, u32[]{:S(2)}) collective-permute-start(f32[96,128]{1,0:T(8,128)S(1)} %add_add_fusion.1), channel_id=1, source_target_pairs={{0,22},{1,23},{2,20},{3,21},{4,18},{5,19},{6,16},{7,17},{16,6},{17... | collective-permute-start | bytes 147464 | tf_op jit(solution)/shard_map/ppermute | solution.py:198
  54.1 0.3 collective-permute-start.15
  54.5 1.7 %collective-permute-start.14 = (f32[96,128]{1,0:T(8,128)S(1)}, f32[96,128]{1,0:T(8,128)S(1)}, u32[]{:S(2)}, u32[]{:S(2)}) collective-permute-start(f32[96,128]{1,0:T(8,128)S(1)} %add_add_fusion.1), channel_id=1, source_target_pairs={{0,6},{1,7},{2,4},{3,5},{4,2},{5,3},{6,0},{7,1},{16,22},{17,23},{1... | collective-permute-start | bytes 147464 | tf_op jit(solution)/shard_map/ppermute | solution.py:198
  56.2 0.0 collective-permute-done.19.r1_ref
  56.2 0.9 %collective-permute-start.20 = (f32[4,5,8,128]{3,2,1,0:T(8,128)S(1)}, f32[4,5,8,128]{3,2,1,0:T(8,128)S(1)}, u32[]{:S(2)}, u32[]{:S(2)}) collective-permute-start(f32[4,5,8,128]{3,2,1,0:T(8,128)S(1)} %pad_maximum_fusion), channel_id=1, source_target_pairs={{0,32},{16,48},{32,0},{48,16},{64,96},{80,112},{96,64},{112,80},{1... | collective-permute-start | bytes 245768 | tf_op jit(solution)/shard_map/ppermute | solution.py:192
  57.1 0.7 collective-permute-done.16
  57.8 0.7 collective-permute-done.15
  58.5 1.3 %collective-permute-done.14 = f32[96,128]{1,0:T(8,128)S(1)} collective-permute-done((f32[96,128]{1,0:T(8,128)S(1)}, f32[96,128]{1,0:T(8,128)S(1)}, u32[]{:S(2)}, u32[]{:S(2)}) %collective-permute-start.14) | collective-permute-done | bytes 49184 | tf_op jit(solution)/shard_map/ppermute | solution.py:198
  59.8 0.9 %collective-permute-start.17 = (f32[96,128]{1,0:T(8,128)S(1)}, f32[96,128]{1,0:T(8,128)S(1)}, u32[]{:S(2)}, u32[]{:S(2)}) collective-permute-start(f32[96,128]{1,0:T(8,128)S(1)} %add_add_fusion), channel_id=1, source_target_pairs={{0,32},{16,48},{32,0},{48,16},{64,96},{80,112},{96,64},{112,80},{1... | collective-permute-start | bytes 147464 | tf_op jit(solution)/shard_map/ppermute | solution.py:192
  60.6 1.0 %collective-permute-done.20.r2_ref = f32[4,5,8,128]{3,2,1,0:T(8,128)S(1)} collective-permute-done((f32[4,5,8,128]{3,2,1,0:T(8,128)S(1)}, f32[4,5,8,128]{3,2,1,0:T(8,128)S(1)}, u32[]{:S(2)}, u32[]{:S(2)}) %collective-permute-start.20) | collective-permute-done | bytes 81952 | tf_op jit(solution)/shard_map/ppermute | solution.py:192
  61.7 1.7 %collective-permute-start.21 = (f32[4,5,8,128]{3,2,1,0:T(8,128)S(1)}, f32[4,5,8,128]{3,2,1,0:T(8,128)S(1)}, u32[]{:S(2)}, u32[]{:S(2)}) collective-permute-start(f32[4,5,8,128]{3,2,1,0:T(8,128)S(1)} %pad_maximum_fusion.1), channel_id=1, source_target_pairs={{0,112},{16,96},{32,80},{48,64},{64,48},{80,32},{96,16},{112,0},{1... | collective-permute-start | bytes 245768 | tf_op jit(solution)/shard_map/ppermute | solution.py:192
  63.4 1.5 %collective-permute-done.17 = f32[96,128]{1,0:T(8,128)S(1)} collective-permute-done((f32[96,128]{1,0:T(8,128)S(1)}, f32[96,128]{1,0:T(8,128)S(1)}, u32[]{:S(2)}, u32[]{:S(2)}) %collective-permute-start.17) | collective-permute-done | bytes 49184 | tf_op jit(solution)/shard_map/ppermute | solution.py:192
  64.9 2.0 %collective-permute-start.18 = (f32[96,128]{1,0:T(8,128)S(1)}, f32[96,128]{1,0:T(8,128)S(1)}, u32[]{:S(2)}, u32[]{:S(2)}) collective-permute-start(f32[96,128]{1,0:T(8,128)S(1)} %add.59.p_ref), channel_id=1, source_target_pairs={{0,112},{16,96},{32,80},{48,64},{64,48},{80,32},{96,16},{112,0},{1... | collective-permute-start | bytes 147464 | tf_op jit(solution)/shard_map/ppermute | solution.py:192
  66.9 5.2 %collective-permute-done.18.q_ref = f32[96,128]{1,0:T(8,128)S(1)} collective-permute-done((f32[96,128]{1,0:T(8,128)S(1)}, f32[96,128]{1,0:T(8,128)S(1)}, u32[]{:S(2)}, u32[]{:S(2)}) %collective-permute-start.18) | collective-permute-done | bytes 49184 | tf_op jit(solution)/shard_map/ppermute | solution.py:192
  72.2 3.5 %shard_map.64 = (f32[64,96]{1,0:T(8,128)}, f32[6,6,6,96]{3,2,1,0:T(8,128)}) custom-call(f32[96,128]{1,0:T(8,128)S(1)} %add.59.p_ref, f32[96,128]{1,0:T(8,128)S(1)} %collective-permute-done.18.q_ref, f32[1,5,8,128]{3,2,1,0:T(8,128)S(1)} %get-tuple-element.22.a0_ref, f32[4,5,8,128]{3,2,1,0:T(8,128)S(1)} %collective-permute-done.19.r1_ref, ...), custom_call_target="tpu_custom_call" | custom-call | tf_op jit(solution)/shard_map/pallas_call | solution.py:181
  (19 shorter events, 0.1 us)
Async XLA Ops:
  0.6 0.7 copy-start.1
  1.4 17.3 %copy-start.2 = (f32[16,96]{1,0:T(8,128)S(1)}, f32[16,96]{1,0:T(8,128)}, u32[]{:S(2)}) copy-start(f32[16,96]{1,0:T(8,128)} %mid_ref.1) | copy-start | bytes 18436
  1.4 34.3 %copy-start = (f32[64,96]{1,0:T(8,128)S(1)}, f32[64,96]{1,0:T(8,128)}, u32[]{:S(2)}) copy-start(f32[64,96]{1,0:T(8,128)} %old_ref.3) | copy-start | bytes 73732
  3.9 1.8 %collective-permute-start = (f32[576,128]{1,0:T(8,128)S(1)}, f32[576,128]{1,0:T(8,128)S(1)}, u32[]{:S(2)}, u32[]{:S(2)}) collective-permute-start(f32[576,128]{1,0:T(8,128)S(1)} %get-tuple-element.15), channel_id=1, source_target_pairs={{0,1},{1,0},{2,3},{3,2},{4,5},{5,4},{6,7},{7,6},{8,9},{9,8},{10,11... | collective-permute-start | bytes 884744 | tf_op jit(solution)/shard_map/ppermute | solution.py:192
  5.1 4.8 %collective-permute-start.4 = (f32[576,128]{1,0:T(8,128)S(1)}, f32[576,128]{1,0:T(8,128)S(1)}, u32[]{:S(2)}, u32[]{:S(2)}) collective-permute-start(f32[576,128]{1,0:T(8,128)S(1)} %get-tuple-element.18), channel_id=1, source_target_pairs={{0,1},{1,0},{2,3},{3,2},{4,5},{5,4},{6,7},{7,6},{8,9},{9,8},{10,11... | collective-permute-start | bytes 884744 | tf_op jit(solution)/shard_map/ppermute | solution.py:192
  5.7 7.9 %collective-permute-start.3 = (f32[144,128]{1,0:T(8,128)S(1)}, f32[144,128]{1,0:T(8,128)S(1)}, u32[]{:S(2)}, u32[]{:S(2)}) collective-permute-start(f32[144,128]{1,0:T(8,128)S(1)} %get-tuple-element.30), channel_id=1, source_target_pairs={{0,6},{2,4},{4,2},{6,0},{1,7},{3,5},{5,3},{7,1},{8,14},{10,12},{12... | collective-permute-start | bytes 221192 | tf_op jit(solution)/shard_map/ppermute | solution.py:192
  8.6 6.2 %collective-permute-start.2 = (f32[144,128]{1,0:T(8,128)S(1)}, f32[144,128]{1,0:T(8,128)S(1)}, u32[]{:S(2)}, u32[]{:S(2)}) collective-permute-start(f32[144,128]{1,0:T(8,128)S(1)} %get-tuple-element.31), channel_id=1, source_target_pairs={{0,4},{2,6},{4,0},{6,2},{1,5},{3,7},{5,1},{7,3},{8,12},{10,14},{12... | collective-permute-start | bytes 221192 | tf_op jit(solution)/shard_map/ppermute | solution.py:192
  9.4 5.4 %collective-permute-start.1 = (f32[144,128]{1,0:T(8,128)S(1)}, f32[144,128]{1,0:T(8,128)S(1)}, u32[]{:S(2)}, u32[]{:S(2)}) collective-permute-start(f32[144,128]{1,0:T(8,128)S(1)} %get-tuple-element.32), channel_id=1, source_target_pairs={{0,2},{2,0},{4,6},{6,4},{1,3},{3,1},{5,7},{7,5},{8,10},{10,8},{12,... | collective-permute-start | bytes 221192 | tf_op jit(solution)/shard_map/ppermute | solution.py:192
  9.9 5.7 %collective-permute-start.7 = (f32[144,128]{1,0:T(8,128)S(1)}, f32[144,128]{1,0:T(8,128)S(1)}, u32[]{:S(2)}, u32[]{:S(2)}) collective-permute-start(f32[144,128]{1,0:T(8,128)S(1)} %get-tuple-element.26), channel_id=1, source_target_pairs={{0,6},{2,4},{4,2},{6,0},{1,7},{3,5},{5,3},{7,1},{8,14},{10,12},{12... | collective-permute-start | bytes 221192 | tf_op jit(solution)/shard_map/ppermute | solution.py:192
  12.8 5.9 %collective-permute-start.6 = (f32[144,128]{1,0:T(8,128)S(1)}, f32[144,128]{1,0:T(8,128)S(1)}, u32[]{:S(2)}, u32[]{:S(2)}) collective-permute-start(f32[144,128]{1,0:T(8,128)S(1)} %get-tuple-element.27), channel_id=1, source_target_pairs={{0,4},{2,6},{4,0},{6,2},{1,5},{3,7},{5,1},{7,3},{8,12},{10,14},{12... | collective-permute-start | bytes 221192 | tf_op jit(solution)/shard_map/ppermute | solution.py:192
  13.6 5.1 %collective-permute-start.5 = (f32[144,128]{1,0:T(8,128)S(1)}, f32[144,128]{1,0:T(8,128)S(1)}, u32[]{:S(2)}, u32[]{:S(2)}) collective-permute-start(f32[144,128]{1,0:T(8,128)S(1)} %get-tuple-element.28), channel_id=1, source_target_pairs={{0,2},{2,0},{4,6},{6,4},{1,3},{3,1},{5,7},{7,5},{8,10},{10,8},{12,... | collective-permute-start | bytes 221192 | tf_op jit(solution)/shard_map/ppermute | solution.py:192
  36.3 9.4 %collective-permute-start.9 = (f32[304,128]{1,0:T(8,128)S(1)}, f32[304,128]{1,0:T(8,128)S(1)}, u32[]{:S(2)}, u32[]{:S(2)}) collective-permute-start(f32[304,128]{1,0:T(8,128)S(1)} %get-tuple-element.20), channel_id=1, source_target_pairs={{0,128},{8,136},{128,0},{136,8},{1,129},{9,137},{129,1},{137,9},{2... | collective-permute-start | bytes 466952 | tf_op jit(solution)/shard_map/ppermute | solution.py:192
  39.6 6.1 %collective-permute-start.10 = (f32[240,128]{1,0:T(8,128)S(1)}, f32[240,128]{1,0:T(8,128)S(1)}, u32[]{:S(2)}, u32[]{:S(2)}) collective-permute-start(f32[240,128]{1,0:T(8,128)S(1)} %get-tuple-element.19.own_ref), channel_id=1, source_target_pairs={{0,136},{8,128},{128,8},{136,0},{1,137},{9,129},{129,9},{137,1},{2... | collective-permute-start | bytes 368648 | tf_op jit(solution)/shard_map/ppermute | solution.py:192
  40.7 5.0 %collective-permute-start.8 = (f32[240,128]{1,0:T(8,128)S(1)}, f32[240,128]{1,0:T(8,128)S(1)}, u32[]{:S(2)}, u32[]{:S(2)}) collective-permute-start(f32[240,128]{1,0:T(8,128)S(1)} %get-tuple-element.19.own_ref), channel_id=1, source_target_pairs={{0,8},{8,0},{128,136},{136,128},{1,9},{9,1},{129,137},{137,129},{2... | collective-permute-start | bytes 368648 | tf_op jit(solution)/shard_map/ppermute | solution.py:192
  46.5 3.7 %collective-permute-start.13 = (f32[96,128]{1,0:T(8,128)S(1)}, f32[96,128]{1,0:T(8,128)S(1)}, u32[]{:S(2)}, u32[]{:S(2)}) collective-permute-start(f32[96,128]{1,0:T(8,128)S(1)} %get-tuple-element.21), channel_id=1, source_target_pairs={{0,3},{1,2},{2,1},{3,0},{4,7},{5,6},{6,5},{7,4},{16,19},{17,18},{1... | collective-permute-start | bytes 147464 | tf_op jit(solution)/shard_map/ppermute | solution.py:198
  46.6 4.6 %collective-permute-start.12 = (f32[96,128]{1,0:T(8,128)S(1)}, f32[96,128]{1,0:T(8,128)S(1)}, u32[]{:S(2)}, u32[]{:S(2)}) collective-permute-start(f32[96,128]{1,0:T(8,128)S(1)} %get-tuple-element.21), channel_id=1, source_target_pairs={{0,2},{1,3},{2,0},{3,1},{4,6},{5,7},{6,4},{7,5},{16,18},{17,19},{1... | collective-permute-start | bytes 147464 | tf_op jit(solution)/shard_map/ppermute | solution.py:198
  46.9 4.2 %collective-permute-start.11 = (f32[96,128]{1,0:T(8,128)S(1)}, f32[96,128]{1,0:T(8,128)S(1)}, u32[]{:S(2)}, u32[]{:S(2)}) collective-permute-start(f32[96,128]{1,0:T(8,128)S(1)} %get-tuple-element.21), channel_id=1, source_target_pairs={{0,1},{1,0},{2,3},{3,2},{4,5},{5,4},{6,7},{7,6},{16,17},{17,16},{1... | collective-permute-start | bytes 147464 | tf_op jit(solution)/shard_map/ppermute | solution.py:198
  48.5 7.7 %collective-permute-start.19 = (f32[4,5,8,128]{3,2,1,0:T(8,128)S(1)}, f32[4,5,8,128]{3,2,1,0:T(8,128)S(1)}, u32[]{:S(2)}, u32[]{:S(2)}) collective-permute-start(f32[4,5,8,128]{3,2,1,0:T(8,128)S(1)} %get-tuple-element.23), channel_id=1, source_target_pairs={{0,16},{16,0},{32,48},{48,32},{64,80},{80,64},{96,112},{112,96},{1... | collective-permute-start | bytes 245768 | tf_op jit(solution)/shard_map/ppermute | solution.py:192
  51.2 6.6 %collective-permute-start.16 = (f32[96,128]{1,0:T(8,128)S(1)}, f32[96,128]{1,0:T(8,128)S(1)}, u32[]{:S(2)}, u32[]{:S(2)}) collective-permute-start(f32[96,128]{1,0:T(8,128)S(1)} %add_add_fusion.1), channel_id=1, source_target_pairs={{0,22},{1,23},{2,20},{3,21},{4,18},{5,19},{6,16},{7,17},{16,6},{17... | collective-permute-start | bytes 147464 | tf_op jit(solution)/shard_map/ppermute | solution.py:198
  54.1 4.4 %collective-permute-start.15 = (f32[96,128]{1,0:T(8,128)S(1)}, f32[96,128]{1,0:T(8,128)S(1)}, u32[]{:S(2)}, u32[]{:S(2)}) collective-permute-start(f32[96,128]{1,0:T(8,128)S(1)} %add_add_fusion.1), channel_id=1, source_target_pairs={{0,16},{1,17},{2,18},{3,19},{4,20},{5,21},{6,22},{7,23},{16,0},{17... | collective-permute-start | bytes 147464 | tf_op jit(solution)/shard_map/ppermute | solution.py:198
  54.5 5.3 %collective-permute-start.14 = (f32[96,128]{1,0:T(8,128)S(1)}, f32[96,128]{1,0:T(8,128)S(1)}, u32[]{:S(2)}, u32[]{:S(2)}) collective-permute-start(f32[96,128]{1,0:T(8,128)S(1)} %add_add_fusion.1), channel_id=1, source_target_pairs={{0,6},{1,7},{2,4},{3,5},{4,2},{5,3},{6,0},{7,1},{16,22},{17,23},{1... | collective-permute-start | bytes 147464 | tf_op jit(solution)/shard_map/ppermute | solution.py:198
  56.2 5.5 %collective-permute-start.20 = (f32[4,5,8,128]{3,2,1,0:T(8,128)S(1)}, f32[4,5,8,128]{3,2,1,0:T(8,128)S(1)}, u32[]{:S(2)}, u32[]{:S(2)}) collective-permute-start(f32[4,5,8,128]{3,2,1,0:T(8,128)S(1)} %pad_maximum_fusion), channel_id=1, source_target_pairs={{0,32},{16,48},{32,0},{48,16},{64,96},{80,112},{96,64},{112,80},{1... | collective-permute-start | bytes 245768 | tf_op jit(solution)/shard_map/ppermute | solution.py:192
  59.8 5.1 %collective-permute-start.17 = (f32[96,128]{1,0:T(8,128)S(1)}, f32[96,128]{1,0:T(8,128)S(1)}, u32[]{:S(2)}, u32[]{:S(2)}) collective-permute-start(f32[96,128]{1,0:T(8,128)S(1)} %add_add_fusion), channel_id=1, source_target_pairs={{0,32},{16,48},{32,0},{48,16},{64,96},{80,112},{96,64},{112,80},{1... | collective-permute-start | bytes 147464 | tf_op jit(solution)/shard_map/ppermute | solution.py:192
  61.7 10.5 %collective-permute-start.21 = (f32[4,5,8,128]{3,2,1,0:T(8,128)S(1)}, f32[4,5,8,128]{3,2,1,0:T(8,128)S(1)}, u32[]{:S(2)}, u32[]{:S(2)}) collective-permute-start(f32[4,5,8,128]{3,2,1,0:T(8,128)S(1)} %pad_maximum_fusion.1), channel_id=1, source_target_pairs={{0,112},{16,96},{32,80},{48,64},{64,48},{80,32},{96,16},{112,0},{1... | collective-permute-start | bytes 245768 | tf_op jit(solution)/shard_map/ppermute | solution.py:192
  64.9 7.3 %collective-permute-start.18 = (f32[96,128]{1,0:T(8,128)S(1)}, f32[96,128]{1,0:T(8,128)S(1)}, u32[]{:S(2)}, u32[]{:S(2)}) collective-permute-start(f32[96,128]{1,0:T(8,128)S(1)} %add.59.p_ref), channel_id=1, source_target_pairs={{0,112},{16,96},{32,80},{48,64},{64,48},{80,32},{96,16},{112,0},{1... | collective-permute-start | bytes 147464 | tf_op jit(solution)/shard_map/ppermute | solution.py:192

commit v4 on v3

--- a/solution.py
+++ b/solution.py
@@ -13,7 +13,7 @@
 PAIRS = 36
 SLOTS = 5
 TILES = 7
-G1, G2, G3 = 1, 2, 7
+G1, G2, G3 = 1, 2, 6
 HALF = SLOTS * 48
 
 
@@ -44,16 +44,19 @@
     return jnp.concatenate([jnp.concatenate([high, high], axis=1), jnp.concatenate([low, low], axis=1)], axis=0)
 
 
-def project_first(vel_ref, deep_ref, send_ref, keep_ref, next_ref, cells_ref, sems):
-    copies = [pltpu.make_async_copy(vel_ref.at[k], cells_ref.at[k], sems.at[k]) for k in range(KP)]
-    copies.append(pltpu.make_async_copy(vel_ref.at[pl.ds(KP, K - KP)], next_ref, sems.at[KP]))
-    for copy in copies:
-        copy.start()
+def fetch(vel_ref, cells_ref, sem):
+    copy = pltpu.make_async_copy(vel_ref.at[pl.ds(0, KP)], cells_ref, sem)
+    copy.start()
+    copy.wait()
+
+
+def project_first(cells_ref, vel_ref, deep_ref, send_ref, keep_ref, next_ref, sem):
+    copy = pltpu.make_async_copy(vel_ref.at[pl.ds(KP, K - KP)], next_ref, sem)
+    copy.start()
     deep = ranks(deep_ref)
     for k in range(KP):
-        copies[k].wait()
         project_cells(k, cells_ref, deep, send_ref, keep_ref)
-    copies[KP].wait()
+    copy.wait()
 
 
 def project_rest(cells_ref, deep_ref, send_ref, keep_ref):
@@ -87,7 +90,12 @@
 def project_mid(got_ref, old_ref, part_ref, more_ref):
     mid = jnp.concatenate([got_ref[:, 5 + par].reshape(64, 128).T[:R1] for par in range(2)], axis=0)
     cells = jnp.concatenate([got_ref[:, slot].reshape(64, 128) for slot in range(SLOTS)], axis=1)
-    both = dot(mid, cells, 1, 0)
+    mid_high, mid_low = halves(mid)
+    left = jnp.concatenate(
+        [jnp.concatenate([mid_high, mid_high], axis=1), jnp.concatenate([mid_low, mid_low], axis=1)], axis=0
+    )
+    both = dot(left, jnp.concatenate(halves(cells), axis=0), 1, 0, None)
+    both = both[:2 * R1] + both[2 * R1:]
     low = lax.broadcasted_iota(jnp.int32, (48, 128), 1) < 64
     for slot in range(SLOTS):
         at = slice(slot * 128, slot * 128 + 128)
@@ -109,8 +117,11 @@
     low = lax.broadcasted_iota(jnp.int32, (HALF, 128), 1) < 64
     p0 = jnp.where(low, h0, pltpu.roll(h1, 64, 1))
     p1 = jnp.where(low, pltpu.roll(h0, 64, 1), h1)
-    stack = jnp.concatenate([p0, p1], axis=0)
-    square = dot(stack, stack, 0, 0)
+    high, low = halves(jnp.concatenate([p0, p1], axis=0))
+    left = jnp.concatenate([high, low], axis=0)
+    right = jnp.concatenate([left, jnp.concatenate([low, high], axis=0)], axis=1)
+    square = dot(left, right, 0, 0, None)
+    square = square[:, :NX] + square[:, NX:]
     other = r2[HALF:HALF + 64, :R1]
     own = old_ref[...]
     old = jnp.concatenate([jnp.where(yh == 0, own, other), jnp.where(yh == 0, other, own)], axis=0)
@@ -157,8 +168,8 @@
     return jnp.concatenate(done, axis=0)
 
 
-def finish(p_ref, q_ref, a0_ref, r1_ref, r2_ref, r3_ref, basis_ref, core_ref, rows_ref, turn_ref):
-    yh, z = lax.axis_index("yh"), lax.axis_index("z")
+def gather_rows(a0_ref, r1_ref, r2_ref, r3_ref, rows_ref):
+    z = lax.axis_index("z")
     held = [(0, a0_ref, 0), (G1, r1_ref, 3), (G2, r2_ref, 0), (G1 ^ G2, r2_ref, 2)]
     held += [(G3 ^ m, r3_ref, i) for i, m in enumerate((0, G1, G2, G1 ^ G2))]
     for m, ref, i in held:
@@ -166,11 +177,20 @@
             pair = (z ^ m) * SLOTS + slot
             at = jnp.where(pair < PAIRS, pair % PP // KP * 8 + pair // PP * KP + pair % KP, 7)
             rows_ref[pl.ds(at, 6, stride=48), :] = ref[i, slot, 0:6, :]
+
+
+def finish(p_ref, q_ref, rows_ref, basis_ref, core_ref, turn_ref):
+    yh = lax.axis_index("yh")
     image_t = p_ref[...] + q_ref[...]
     basis_t = solve(dot(image_t, image_t, 1, 1), image_t)
     turn_ref[...] = basis_t.T
     basis_ref[...] = turn_ref[pl.ds(pl.multiple_of(yh * 64, 64), 64), :]
-    core = dot(rows_ref[...], basis_t, 1, 1)
+    high, low = halves(jnp.concatenate([basis_t, jnp.zeros((128 - R1, NX), F32)], axis=0))
+    right = jnp.concatenate(
+        [jnp.concatenate([high, high], axis=1), jnp.concatenate([low, low], axis=1)], axis=0
+    )
+    core = dot(jnp.concatenate(halves(rows_ref[...]), axis=1), right, 1, 1, None)
+    core = core[:, :R1] + core[:, 128:128 + R1]
     core_ref[...] = core.reshape(6, 6, 8, R1)[:, :, :6, :]
 
 
@@ -207,14 +227,24 @@
 def on_device(velocity, basis_old, basis_mid, basis_deep):
     deep = basis_deep.T
     parts = [(XS * PP * 8, 128)] * 2
+    block = (KP, 64, 16, 128)
+    limit = pltpu.CompilerParams(vmem_limit_bytes=50 * 2**20)
+    cells = pl.pallas_call(
+        fetch,
+        out_shape=jax.ShapeDtypeStruct(block, F32),
+        in_specs=[pl.BlockSpec(memory_space=pltpu.HBM)],
+        out_specs=VMEM,
+        scratch_shapes=[pltpu.SemaphoreType.DMA],
+        compiler_params=limit,
+    )(velocity)
     send, keep, cells = pl.pallas_call(
         project_first,
-        out_shape=[jax.ShapeDtypeStruct(s, F32) for s in (*parts, (K - KP, 64, 16, 128))],
-        in_specs=[pl.BlockSpec(memory_space=pltpu.HBM), VMEM],
+        out_shape=[jax.ShapeDtypeStruct(s, F32) for s in (*parts, block)],
+        in_specs=[VMEM, pl.BlockSpec(memory_space=pltpu.HBM), VMEM],
         out_specs=[VMEM] * 3,
-        scratch_shapes=[pltpu.VMEM((KP, 64, 16, 128), F32), pltpu.SemaphoreType.DMA((KP + 1,))],
-        compiler_params=pltpu.CompilerParams(vmem_limit_bytes=51 * 2**20),
-    )(velocity, deep)
+        scratch_shapes=[pltpu.SemaphoreType.DMA],
+        compiler_params=limit,
+    )(cells, velocity, deep)
     sums = []
     for part in range(2):
         if part:
@@ -238,15 +268,16 @@
     b1 = swap(a1, "z", ZS, G1)
     b2 = swap(jnp.concatenate([a2, b1[:2]]), "z", ZS, G2)
     b3 = swap(jnp.concatenate([a3, b1[2:3], b2[1:2], b2[3:4]]), "z", ZS, G3)
-    image = across(image, 1, 2)
-    image = across(image, 6, 8)
-    image = image + swap(image, "z", 8, 2)
-    last = swap(image, "z", ZS, 7)
+    image = across(image, 1, 8)
+    image = across(image, 2, 6)
+    image = image + swap(image, "z", ZS, 6)
+    last = swap(image, "z", ZS, 2)
+    (rows,) = call(gather_rows, [(288, 128)], a0, b1, b2, b3)
     basis_new, core_block = call(
         finish,
         [(64, R1), (6, 6, 6, R1)],
-        image, last, a0, b1, b2, b3,
-        scratch=[(288, 128), (NX, R1)],
+        image, last, rows,
+        scratch=[(NX, R1)],
     )
     return (basis_new, core_block)
 

time: 75.9 us -> 74.6 us (0.983)
  starting transfers between devices: 27.5 us -> 25.1 us
  waiting for transfers between devices: 21 us -> 22.8 us
    pallas_call x0 -> x1, Pallas kernels: none -> 1.42 us  [on_device(): pl.pallas_call(fetch, out_shape=jax.ShapeDtypeStruct(block, F32), in_spec...]
    ppermute x6, starting transfers between devices: 6.91 us -> 5.53 us  [across(): lax.ppermute(value, axes, [(i, i ^ m) for i in range(ZS * XS * CORES)])]
    ppermute x16, waiting for transfers between devices: 17.4 us -> 18.7 us  [swap(): return lax.ppermute(value, axis, [(i, i ^ bit) for i in range(size)])]
    ppermute x16, starting transfers between devices: 20.6 us -> 19.6 us  [swap(): return lax.ppermute(value, axis, [(i, i ^ bit) for i in range(size)])]
    pallas_call x1, Pallas kernels: 2.48 us -> 1.6 us  [on_device(): pl.pallas_call(project_first, out_shape=[jax.ShapeDtypeStruct(s, F32) for...]
    pallas_call x5 -> x6, Pallas kernels: 6.35 us -> 5.81 us  [call(): pl.pallas_call(kernel, out_shape=[jax.ShapeDtypeStruct(s, F32) for s in o...]
  transfers between devices with their start and end apart: 22 -> 22, of which waited for: 11 -> 12; matrix products, arithmetic and copies ran while one was open for 0% -> 0% of each run, Pallas kernels for 1% -> 2%
where the time goes in v4:
time: 74.6 us; the launch traced here: 74.4 us
  starting transfers between devices  25.1 us (34%)
  waiting for transfers between devices  22.8 us (31%)
  blocking collectives  16.8 us (23%)
  Pallas kernels  8.83 us (12%)
  between operations  0.78 us (1%)
    ppermute x16, starting transfers between devices, swap(): return lax.ppermute(value, axis, [(i, i ^ bit) for i in range(size)])  19.6 us
    ppermute x16, waiting for transfers between devices, swap(): return lax.ppermute(value, axis, [(i, i ^ bit) for i in range(size)])  18.7 us
    all_to_all x1, blocking collectives, on_device(): mine = lax.all_to_all(packed, 'z', 0, 0, tiled=True)  16.8 us
    pallas_call x6, Pallas kernels, call(): pl.pallas_call(kernel, out_shape=[jax.ShapeDtypeStruct(s, F32) for s in o...  5.81 us
    ppermute x6, starting transfers between devices, across(): lax.ppermute(value, axes, [(i, i ^ m) for i in range(ZS * XS * CORES)])  5.53 us
    ppermute x6, waiting for transfers between devices, across(): lax.ppermute(value, axes, [(i, i ^ m) for i in range(ZS * XS * CORES)])  4.08 us
    pallas_call x1, Pallas kernels, on_device(): pl.pallas_call(project_first, out_shape=[jax.ShapeDtypeStruct(s, F32) for...  1.6 us
  transfers between devices with their start and end apart: 22, of which 12 were waited for; matrix products, arithmetic and copies ran while one was open for 0% of the time, Pallas kernels for 2%

profile of v4, /device:TPU:32, one launch (start us, length us, event | category | flops | bytes accessed | tf_op | source)
XLA Modules:
  0.0 74.4 jit_solution(15741817088004110901)
XLA Ops:
  0.6 1.4 %shard_map.59.cells_ref = f32[3,64,16,128]{3,2,1,0:T(8,128)S(1)} custom-call(f32[6,64,16,128]{3,2,1,0:T(8,128)} %vel_ref.3), custom_call_target="tpu_custom_call" | custom-call | tf_op jit(solution)/shard_map/pallas_call | solution.py:232
  2.1 1.6 %shard_map.60 = (f32[576,128]{1,0:T(8,128)S(1)}, f32[576,128]{1,0:T(8,128)S(1)}, f32[3,64,16,128]{3,2,1,0:T(8,128)S(1)}) custom-call(f32[3,64,16,128]{3,2,1,0:T(8,128)S(1)} %shard_map.59.cells_ref, f32[6,64,16,128]{3,2,1,0:T(8,128)} %vel_ref.3, f32[48,128]{1,0:T(8,128)S(1)} %bitcast.1), custom_call_target="tpu_custom_call" | custom-call | tf_op jit(solution)/shard_map/pallas_call | solution.py:240
  3.7 0.1 collective-permute-start
  3.8 0.0 copy-start.2
  3.8 1.1 %shard_map.61 = (f32[576,128]{1,0:T(8,128)S(1)}, f32[576,128]{1,0:T(8,128)S(1)}) custom-call(f32[3,64,16,128]{3,2,1,0:T(8,128)S(1)} %get-tuple-element.16.cells_ref, f32[48,128]{1,0:T(8,128)S(1)} %bitcast.2), custom_call_target="tpu_custom_call" | custom-call | tf_op jit(solution)/shard_map/pallas_call | solution.py:201
  4.9 0.0 copy-start
  4.9 0.6 collective-permute-start.4
  5.6 2.8 %collective-permute-start.3 = (f32[144,128]{1,0:T(8,128)S(1)}, f32[144,128]{1,0:T(8,128)S(1)}, u32[]{:S(2)}, u32[]{:S(2)}) collective-permute-start(f32[144,128]{1,0:T(8,128)S(1)} %get-tuple-element.30), channel_id=1, source_target_pairs={{0,6},{2,4},{4,2},{6,0},{1,7},{3,5},{5,3},{7,1},{8,14},{10,12},{12... | collective-permute-start | bytes 221192 | tf_op jit(solution)/shard_map/ppermute | solution.py:212
  8.4 0.8 %collective-permute-start.2 = (f32[144,128]{1,0:T(8,128)S(1)}, f32[144,128]{1,0:T(8,128)S(1)}, u32[]{:S(2)}, u32[]{:S(2)}) collective-permute-start(f32[144,128]{1,0:T(8,128)S(1)} %get-tuple-element.31), channel_id=1, source_target_pairs={{0,4},{2,6},{4,0},{6,2},{1,5},{3,7},{5,1},{7,3},{8,12},{10,14},{12... | collective-permute-start | bytes 221192 | tf_op jit(solution)/shard_map/ppermute | solution.py:212
  9.2 0.5 collective-permute-start.1
  9.7 0.0 collective-permute-done.4
  9.8 2.8 %collective-permute-start.7 = (f32[144,128]{1,0:T(8,128)S(1)}, f32[144,128]{1,0:T(8,128)S(1)}, u32[]{:S(2)}, u32[]{:S(2)}) collective-permute-start(f32[144,128]{1,0:T(8,128)S(1)} %get-tuple-element.26), channel_id=1, source_target_pairs={{0,6},{2,4},{4,2},{6,0},{1,7},{3,5},{5,3},{7,1},{8,14},{10,12},{12... | collective-permute-start | bytes 221192 | tf_op jit(solution)/shard_map/ppermute | solution.py:212
  12.6 0.8 %collective-permute-start.6 = (f32[144,128]{1,0:T(8,128)S(1)}, f32[144,128]{1,0:T(8,128)S(1)}, u32[]{:S(2)}, u32[]{:S(2)}) collective-permute-start(f32[144,128]{1,0:T(8,128)S(1)} %get-tuple-element.27), channel_id=1, source_target_pairs={{0,4},{2,6},{4,0},{6,2},{1,5},{3,7},{5,1},{7,3},{8,12},{10,14},{12... | collective-permute-start | bytes 221192 | tf_op jit(solution)/shard_map/ppermute | solution.py:212
  13.4 0.0 collective-permute-done.3.d0
  13.4 0.5 collective-permute-start.5
  14.0 0.7 collective-permute-done.2.c0
  14.6 0.0 collective-permute-done.1.b0
  14.6 0.8 %collective-permute-done.7.d1 = f32[144,128]{1,0:T(8,128)S(1)} collective-permute-done((f32[144,128]{1,0:T(8,128)S(1)}, f32[144,128]{1,0:T(8,128)S(1)}, u32[]{:S(2)}, u32[]{:S(2)}) %collective-permute-start.7) | collective-permute-done | bytes 73760 | tf_op jit(solution)/shard_map/ppermute | solution.py:212
  15.4 3.1 %collective-permute-done.6.c1 = f32[144,128]{1,0:T(8,128)S(1)} collective-permute-done((f32[144,128]{1,0:T(8,128)S(1)}, f32[144,128]{1,0:T(8,128)S(1)}, u32[]{:S(2)}, u32[]{:S(2)}) %collective-permute-start.6) | collective-permute-done | bytes 73760 | tf_op jit(solution)/shard_map/ppermute | solution.py:212
  18.5 0.2 shard_map.62
  18.7 16.8 %all_to_all.5.got_ref = f32[8,7,8,128]{3,2,1,0:T(8,128)S(1)} all-to-all(f32[8,7,8,128]{3,2,1,0:T(8,128)S(1)} %shard_map.62), channel_id=1, replica_groups=mesh['yh'=2,'z'=8,'yl'=2,'x'=4,'core'=2] {'z'}, dimensions={0} | all-to-all | bytes 458752 | tf_op jit(solution)/shard_map/all_to_all | solution.py:258
  35.5 0.5 shard_map.63
  36.0 3.3 %collective-permute-start.9 = (f32[304,128]{1,0:T(8,128)S(1)}, f32[304,128]{1,0:T(8,128)S(1)}, u32[]{:S(2)}, u32[]{:S(2)}) collective-permute-start(f32[304,128]{1,0:T(8,128)S(1)} %get-tuple-element.20), channel_id=1, source_target_pairs={{0,128},{8,136},{128,0},{136,8},{1,129},{9,137},{129,1},{137,9},{2... | collective-permute-start | bytes 466952 | tf_op jit(solution)/shard_map/ppermute | solution.py:212
  39.3 1.1 %collective-permute-start.10 = (f32[240,128]{1,0:T(8,128)S(1)}, f32[240,128]{1,0:T(8,128)S(1)}, u32[]{:S(2)}, u32[]{:S(2)}) collective-permute-start(f32[240,128]{1,0:T(8,128)S(1)} %get-tuple-element.19.own_ref), channel_id=1, source_target_pairs={{0,136},{8,128},{128,8},{136,0},{1,137},{9,129},{129,9},{137,1},{2... | collective-permute-start | bytes 368648 | tf_op jit(solution)/shard_map/ppermute | solution.py:212
  40.3 5.0 %collective-permute-done.10.r3 = f32[240,128]{1,0:T(8,128)S(1)} collective-permute-done((f32[240,128]{1,0:T(8,128)S(1)}, f32[240,128]{1,0:T(8,128)S(1)}, u32[]{:S(2)}, u32[]{:S(2)}) %collective-permute-start.10) | collective-permute-done | bytes 122912 | tf_op jit(solution)/shard_map/ppermute | solution.py:212
  45.4 0.6 shard_map.64
  46.0 0.1 collective-permute-start.13
  46.1 1.8 %collective-permute-start.12 = (f32[96,128]{1,0:T(8,128)S(1)}, f32[96,128]{1,0:T(8,128)S(1)}, u32[]{:S(2)}, u32[]{:S(2)}) collective-permute-start(f32[96,128]{1,0:T(8,128)S(1)} %get-tuple-element.21), channel_id=1, source_target_pairs={{0,16},{1,17},{2,18},{3,19},{4,20},{5,21},{6,22},{7,23},{16,0},{17... | collective-permute-start | bytes 147464 | tf_op jit(solution)/shard_map/ppermute | solution.py:218
  47.9 0.1 collective-permute-start.11
  47.9 1.7 %collective-permute-start.19 = (f32[4,5,8,128]{3,2,1,0:T(8,128)S(1)}, f32[4,5,8,128]{3,2,1,0:T(8,128)S(1)}, u32[]{:S(2)}, u32[]{:S(2)}) collective-permute-start(f32[4,5,8,128]{3,2,1,0:T(8,128)S(1)} %get-tuple-element.23), channel_id=1, source_target_pairs={{0,16},{16,0},{32,48},{48,32},{64,80},{80,64},{96,112},{112,96},{1... | collective-permute-start | bytes 245768 | tf_op jit(solution)/shard_map/ppermute | solution.py:212
  49.6 0.2 collective-permute-done.13
  49.8 0.9 %collective-permute-done.12 = f32[96,128]{1,0:T(8,128)S(1)} collective-permute-done((f32[96,128]{1,0:T(8,128)S(1)}, f32[96,128]{1,0:T(8,128)S(1)}, u32[]{:S(2)}, u32[]{:S(2)}) %collective-permute-start.12) | collective-permute-done | bytes 49184 | tf_op jit(solution)/shard_map/ppermute | solution.py:218
  50.8 2.1 %collective-permute-start.16 = (f32[96,128]{1,0:T(8,128)S(1)}, f32[96,128]{1,0:T(8,128)S(1)}, u32[]{:S(2)}, u32[]{:S(2)}) collective-permute-start(f32[96,128]{1,0:T(8,128)S(1)} %add_add_fusion.1), channel_id=1, source_target_pairs={{0,4},{1,5},{2,6},{3,7},{4,0},{5,1},{6,2},{7,3},{16,20},{17,21},{1... | collective-permute-start | bytes 147464 | tf_op jit(solution)/shard_map/ppermute | solution.py:218
  52.9 0.8 %collective-permute-start.15 = (f32[96,128]{1,0:T(8,128)S(1)}, f32[96,128]{1,0:T(8,128)S(1)}, u32[]{:S(2)}, u32[]{:S(2)}) collective-permute-start(f32[96,128]{1,0:T(8,128)S(1)} %add_add_fusion.1), channel_id=1, source_target_pairs={{0,6},{1,7},{2,4},{3,5},{4,2},{5,3},{6,0},{7,1},{16,22},{17,23},{1... | collective-permute-start | bytes 147464 | tf_op jit(solution)/shard_map/ppermute | solution.py:218
  53.7 0.6 collective-permute-start.14
  54.3 0.0 collective-permute-done.19.r1_ref
  54.4 0.9 %collective-permute-start.20 = (f32[4,5,8,128]{3,2,1,0:T(8,128)S(1)}, f32[4,5,8,128]{3,2,1,0:T(8,128)S(1)}, u32[]{:S(2)}, u32[]{:S(2)}) collective-permute-start(f32[4,5,8,128]{3,2,1,0:T(8,128)S(1)} %pad_maximum_fusion), channel_id=1, source_target_pairs={{0,32},{16,48},{32,0},{48,16},{64,96},{80,112},{96,64},{112,80},{1... | collective-permute-start | bytes 245768 | tf_op jit(solution)/shard_map/ppermute | solution.py:212
  55.2 1.2 %collective-permute-done.16 = f32[96,128]{1,0:T(8,128)S(1)} collective-permute-done((f32[96,128]{1,0:T(8,128)S(1)}, f32[96,128]{1,0:T(8,128)S(1)}, u32[]{:S(2)}, u32[]{:S(2)}) %collective-permute-start.16) | collective-permute-done | bytes 49184 | tf_op jit(solution)/shard_map/ppermute | solution.py:218
  56.4 1.8 %collective-permute-done.15 = f32[96,128]{1,0:T(8,128)S(1)} collective-permute-done((f32[96,128]{1,0:T(8,128)S(1)}, f32[96,128]{1,0:T(8,128)S(1)}, u32[]{:S(2)}, u32[]{:S(2)}) %collective-permute-start.15) | collective-permute-done | bytes 49184 | tf_op jit(solution)/shard_map/ppermute | solution.py:218
  58.2 0.9 %collective-permute-start.17 = (f32[96,128]{1,0:T(8,128)S(1)}, f32[96,128]{1,0:T(8,128)S(1)}, u32[]{:S(2)}, u32[]{:S(2)}) collective-permute-start(f32[96,128]{1,0:T(8,128)S(1)} %add_add_fusion), channel_id=1, source_target_pairs={{0,96},{16,112},{32,64},{48,80},{64,32},{80,48},{96,0},{112,16},{1... | collective-permute-start | bytes 147464 | tf_op jit(solution)/shard_map/ppermute | solution.py:212
  59.1 0.8 %collective-permute-done.20.r2_ref = f32[4,5,8,128]{3,2,1,0:T(8,128)S(1)} collective-permute-done((f32[4,5,8,128]{3,2,1,0:T(8,128)S(1)}, f32[4,5,8,128]{3,2,1,0:T(8,128)S(1)}, u32[]{:S(2)}, u32[]{:S(2)}) %collective-permute-start.20) | collective-permute-done | bytes 81952 | tf_op jit(solution)/shard_map/ppermute | solution.py:212
  59.9 2.6 %collective-permute-start.21 = (f32[4,5,8,128]{3,2,1,0:T(8,128)S(1)}, f32[4,5,8,128]{3,2,1,0:T(8,128)S(1)}, u32[]{:S(2)}, u32[]{:S(2)}) collective-permute-start(f32[4,5,8,128]{3,2,1,0:T(8,128)S(1)} %pad_maximum_fusion.1), channel_id=1, source_target_pairs={{0,96},{16,112},{32,64},{48,80},{64,32},{80,48},{96,0},{112,16},{1... | collective-permute-start | bytes 245768 | tf_op jit(solution)/shard_map/ppermute | solution.py:212
  62.5 3.5 %collective-permute-done.17 = f32[96,128]{1,0:T(8,128)S(1)} collective-permute-done((f32[96,128]{1,0:T(8,128)S(1)}, f32[96,128]{1,0:T(8,128)S(1)}, u32[]{:S(2)}, u32[]{:S(2)}) %collective-permute-start.17) | collective-permute-done | bytes 49184 | tf_op jit(solution)/shard_map/ppermute | solution.py:212
  66.1 0.1 collective-permute-start.18
  66.2 0.8 %collective-permute-done.21.r3_ref = f32[4,5,8,128]{3,2,1,0:T(8,128)S(1)} collective-permute-done((f32[4,5,8,128]{3,2,1,0:T(8,128)S(1)}, f32[4,5,8,128]{3,2,1,0:T(8,128)S(1)}, u32[]{:S(2)}, u32[]{:S(2)}) %collective-permute-start.21) | collective-permute-done | bytes 81952 | tf_op jit(solution)/shard_map/ppermute | solution.py:212
  66.9 0.1 shard_map.65.rows_ref
  67.0 4.1 %collective-permute-done.18.q_ref = f32[96,128]{1,0:T(8,128)S(1)} collective-permute-done((f32[96,128]{1,0:T(8,128)S(1)}, f32[96,128]{1,0:T(8,128)S(1)}, u32[]{:S(2)}, u32[]{:S(2)}) %collective-permute-start.18) | collective-permute-done | bytes 49184 | tf_op jit(solution)/shard_map/ppermute | solution.py:212
  71.1 3.3 %shard_map.66 = (f32[64,96]{1,0:T(8,128)}, f32[6,6,6,96]{3,2,1,0:T(8,128)}) custom-call(f32[96,128]{1,0:T(8,128)S(1)} %add.59.p_ref, f32[96,128]{1,0:T(8,128)S(1)} %collective-permute-done.18.q_ref, f32[288,128]{1,0:T(8,128)S(1)} %shard_map.65.rows_ref), custom_call_target="tpu_custom_call" | custom-call | tf_op jit(solution)/shard_map/pallas_call | solution.py:201
  (21 shorter events, 0.1 us)
Async XLA Ops:
  0.6 1.4 %copy-start.1 = (f32[128,48]{0,1:T(8,128)S(1)}, f32[128,48]{0,1:T(8,128)}, u32[]{:S(2)}) copy-start(f32[128,48]{0,1:T(8,128)} %param.7) | copy-start | bytes 73732
  3.7 1.8 %collective-permute-start = (f32[576,128]{1,0:T(8,128)S(1)}, f32[576,128]{1,0:T(8,128)S(1)}, u32[]{:S(2)}, u32[]{:S(2)}) collective-permute-start(f32[576,128]{1,0:T(8,128)S(1)} %get-tuple-element.15), channel_id=1, source_target_pairs={{0,1},{1,0},{2,3},{3,2},{4,5},{5,4},{6,7},{7,6},{8,9},{9,8},{10,11... | collective-permute-start | bytes 884744 | tf_op jit(solution)/shard_map/ppermute | solution.py:212
  3.8 14.7 %copy-start.2 = (f32[16,96]{1,0:T(8,128)S(1)}, f32[16,96]{1,0:T(8,128)}, u32[]{:S(2)}) copy-start(f32[16,96]{1,0:T(8,128)} %mid_ref.1) | copy-start | bytes 18436
  4.9 30.6 %copy-start = (f32[64,96]{1,0:T(8,128)S(1)}, f32[64,96]{1,0:T(8,128)}, u32[]{:S(2)}) copy-start(f32[64,96]{1,0:T(8,128)} %old_ref.3) | copy-start | bytes 73732
  4.9 4.8 %collective-permute-start.4 = (f32[576,128]{1,0:T(8,128)S(1)}, f32[576,128]{1,0:T(8,128)S(1)}, u32[]{:S(2)}, u32[]{:S(2)}) collective-permute-start(f32[576,128]{1,0:T(8,128)S(1)} %get-tuple-element.18), channel_id=1, source_target_pairs={{0,1},{1,0},{2,3},{3,2},{4,5},{5,4},{6,7},{7,6},{8,9},{9,8},{10,11... | collective-permute-start | bytes 884744 | tf_op jit(solution)/shard_map/ppermute | solution.py:212
  5.6 7.9 %collective-permute-start.3 = (f32[144,128]{1,0:T(8,128)S(1)}, f32[144,128]{1,0:T(8,128)S(1)}, u32[]{:S(2)}, u32[]{:S(2)}) collective-permute-start(f32[144,128]{1,0:T(8,128)S(1)} %get-tuple-element.30), channel_id=1, source_target_pairs={{0,6},{2,4},{4,2},{6,0},{1,7},{3,5},{5,3},{7,1},{8,14},{10,12},{12... | collective-permute-start | bytes 221192 | tf_op jit(solution)/shard_map/ppermute | solution.py:212
  8.4 6.2 %collective-permute-start.2 = (f32[144,128]{1,0:T(8,128)S(1)}, f32[144,128]{1,0:T(8,128)S(1)}, u32[]{:S(2)}, u32[]{:S(2)}) collective-permute-start(f32[144,128]{1,0:T(8,128)S(1)} %get-tuple-element.31), channel_id=1, source_target_pairs={{0,4},{2,6},{4,0},{6,2},{1,5},{3,7},{5,1},{7,3},{8,12},{10,14},{12... | collective-permute-start | bytes 221192 | tf_op jit(solution)/shard_map/ppermute | solution.py:212
  9.2 5.4 %collective-permute-start.1 = (f32[144,128]{1,0:T(8,128)S(1)}, f32[144,128]{1,0:T(8,128)S(1)}, u32[]{:S(2)}, u32[]{:S(2)}) collective-permute-start(f32[144,128]{1,0:T(8,128)S(1)} %get-tuple-element.32), channel_id=1, source_target_pairs={{0,2},{2,0},{4,6},{6,4},{1,3},{3,1},{5,7},{7,5},{8,10},{10,8},{12,... | collective-permute-start | bytes 221192 | tf_op jit(solution)/shard_map/ppermute | solution.py:212
  9.8 5.7 %collective-permute-start.7 = (f32[144,128]{1,0:T(8,128)S(1)}, f32[144,128]{1,0:T(8,128)S(1)}, u32[]{:S(2)}, u32[]{:S(2)}) collective-permute-start(f32[144,128]{1,0:T(8,128)S(1)} %get-tuple-element.26), channel_id=1, source_target_pairs={{0,6},{2,4},{4,2},{6,0},{1,7},{3,5},{5,3},{7,1},{8,14},{10,12},{12... | collective-permute-start | bytes 221192 | tf_op jit(solution)/shard_map/ppermute | solution.py:212
  12.6 5.9 %collective-permute-start.6 = (f32[144,128]{1,0:T(8,128)S(1)}, f32[144,128]{1,0:T(8,128)S(1)}, u32[]{:S(2)}, u32[]{:S(2)}) collective-permute-start(f32[144,128]{1,0:T(8,128)S(1)} %get-tuple-element.27), channel_id=1, source_target_pairs={{0,4},{2,6},{4,0},{6,2},{1,5},{3,7},{5,1},{7,3},{8,12},{10,14},{12... | collective-permute-start | bytes 221192 | tf_op jit(solution)/shard_map/ppermute | solution.py:212
  13.4 5.1 %collective-permute-start.5 = (f32[144,128]{1,0:T(8,128)S(1)}, f32[144,128]{1,0:T(8,128)S(1)}, u32[]{:S(2)}, u32[]{:S(2)}) collective-permute-start(f32[144,128]{1,0:T(8,128)S(1)} %get-tuple-element.28), channel_id=1, source_target_pairs={{0,2},{2,0},{4,6},{6,4},{1,3},{3,1},{5,7},{7,5},{8,10},{10,8},{12,... | collective-permute-start | bytes 221192 | tf_op jit(solution)/shard_map/ppermute | solution.py:212
  36.0 9.4 %collective-permute-start.9 = (f32[304,128]{1,0:T(8,128)S(1)}, f32[304,128]{1,0:T(8,128)S(1)}, u32[]{:S(2)}, u32[]{:S(2)}) collective-permute-start(f32[304,128]{1,0:T(8,128)S(1)} %get-tuple-element.20), channel_id=1, source_target_pairs={{0,128},{8,136},{128,0},{136,8},{1,129},{9,137},{129,1},{137,9},{2... | collective-permute-start | bytes 466952 | tf_op jit(solution)/shard_map/ppermute | solution.py:212
  39.3 6.1 %collective-permute-start.10 = (f32[240,128]{1,0:T(8,128)S(1)}, f32[240,128]{1,0:T(8,128)S(1)}, u32[]{:S(2)}, u32[]{:S(2)}) collective-permute-start(f32[240,128]{1,0:T(8,128)S(1)} %get-tuple-element.19.own_ref), channel_id=1, source_target_pairs={{0,136},{8,128},{128,8},{136,0},{1,137},{9,129},{129,9},{137,1},{2... | collective-permute-start | bytes 368648 | tf_op jit(solution)/shard_map/ppermute | solution.py:212
  40.3 5.0 %collective-permute-start.8 = (f32[240,128]{1,0:T(8,128)S(1)}, f32[240,128]{1,0:T(8,128)S(1)}, u32[]{:S(2)}, u32[]{:S(2)}) collective-permute-start(f32[240,128]{1,0:T(8,128)S(1)} %get-tuple-element.19.own_ref), channel_id=1, source_target_pairs={{0,8},{8,0},{128,136},{136,128},{1,9},{9,1},{129,137},{137,129},{2... | collective-permute-start | bytes 368648 | tf_op jit(solution)/shard_map/ppermute | solution.py:212
  46.0 3.9 %collective-permute-start.13 = (f32[96,128]{1,0:T(8,128)S(1)}, f32[96,128]{1,0:T(8,128)S(1)}, u32[]{:S(2)}, u32[]{:S(2)}) collective-permute-start(f32[96,128]{1,0:T(8,128)S(1)} %get-tuple-element.21), channel_id=1, source_target_pairs={{0,17},{1,16},{2,19},{3,18},{4,21},{5,20},{6,23},{7,22},{16,1},{17... | collective-permute-start | bytes 147464 | tf_op jit(solution)/shard_map/ppermute | solution.py:218
  46.1 4.7 %collective-permute-start.12 = (f32[96,128]{1,0:T(8,128)S(1)}, f32[96,128]{1,0:T(8,128)S(1)}, u32[]{:S(2)}, u32[]{:S(2)}) collective-permute-start(f32[96,128]{1,0:T(8,128)S(1)} %get-tuple-element.21), channel_id=1, source_target_pairs={{0,16},{1,17},{2,18},{3,19},{4,20},{5,21},{6,22},{7,23},{16,0},{17... | collective-permute-start | bytes 147464 | tf_op jit(solution)/shard_map/ppermute | solution.py:218
  47.9 2.9 %collective-permute-start.11 = (f32[96,128]{1,0:T(8,128)S(1)}, f32[96,128]{1,0:T(8,128)S(1)}, u32[]{:S(2)}, u32[]{:S(2)}) collective-permute-start(f32[96,128]{1,0:T(8,128)S(1)} %get-tuple-element.21), channel_id=1, source_target_pairs={{0,1},{1,0},{2,3},{3,2},{4,5},{5,4},{6,7},{7,6},{16,17},{17,16},{1... | collective-permute-start | bytes 147464 | tf_op jit(solution)/shard_map/ppermute | solution.py:218
  47.9 6.4 %collective-permute-start.19 = (f32[4,5,8,128]{3,2,1,0:T(8,128)S(1)}, f32[4,5,8,128]{3,2,1,0:T(8,128)S(1)}, u32[]{:S(2)}, u32[]{:S(2)}) collective-permute-start(f32[4,5,8,128]{3,2,1,0:T(8,128)S(1)} %get-tuple-element.23), channel_id=1, source_target_pairs={{0,16},{16,0},{32,48},{48,32},{64,80},{80,64},{96,112},{112,96},{1... | collective-permute-start | bytes 245768 | tf_op jit(solution)/shard_map/ppermute | solution.py:212
  50.8 5.7 %collective-permute-start.16 = (f32[96,128]{1,0:T(8,128)S(1)}, f32[96,128]{1,0:T(8,128)S(1)}, u32[]{:S(2)}, u32[]{:S(2)}) collective-permute-start(f32[96,128]{1,0:T(8,128)S(1)} %add_add_fusion.1), channel_id=1, source_target_pairs={{0,4},{1,5},{2,6},{3,7},{4,0},{5,1},{6,2},{7,3},{16,20},{17,21},{1... | collective-permute-start | bytes 147464 | tf_op jit(solution)/shard_map/ppermute | solution.py:218
  52.9 5.3 %collective-permute-start.15 = (f32[96,128]{1,0:T(8,128)S(1)}, f32[96,128]{1,0:T(8,128)S(1)}, u32[]{:S(2)}, u32[]{:S(2)}) collective-permute-start(f32[96,128]{1,0:T(8,128)S(1)} %add_add_fusion.1), channel_id=1, source_target_pairs={{0,6},{1,7},{2,4},{3,5},{4,2},{5,3},{6,0},{7,1},{16,22},{17,23},{1... | collective-permute-start | bytes 147464 | tf_op jit(solution)/shard_map/ppermute | solution.py:218
  53.7 4.5 %collective-permute-start.14 = (f32[96,128]{1,0:T(8,128)S(1)}, f32[96,128]{1,0:T(8,128)S(1)}, u32[]{:S(2)}, u32[]{:S(2)}) collective-permute-start(f32[96,128]{1,0:T(8,128)S(1)} %add_add_fusion.1), channel_id=1, source_target_pairs={{0,2},{1,3},{2,0},{3,1},{4,6},{5,7},{6,4},{7,5},{16,18},{17,19},{1... | collective-permute-start | bytes 147464 | tf_op jit(solution)/shard_map/ppermute | solution.py:218
  54.4 5.5 %collective-permute-start.20 = (f32[4,5,8,128]{3,2,1,0:T(8,128)S(1)}, f32[4,5,8,128]{3,2,1,0:T(8,128)S(1)}, u32[]{:S(2)}, u32[]{:S(2)}) collective-permute-start(f32[4,5,8,128]{3,2,1,0:T(8,128)S(1)} %pad_maximum_fusion), channel_id=1, source_target_pairs={{0,32},{16,48},{32,0},{48,16},{64,96},{80,112},{96,64},{112,80},{1... | collective-permute-start | bytes 245768 | tf_op jit(solution)/shard_map/ppermute | solution.py:212
  58.2 7.8 %collective-permute-start.17 = (f32[96,128]{1,0:T(8,128)S(1)}, f32[96,128]{1,0:T(8,128)S(1)}, u32[]{:S(2)}, u32[]{:S(2)}) collective-permute-start(f32[96,128]{1,0:T(8,128)S(1)} %add_add_fusion), channel_id=1, source_target_pairs={{0,96},{16,112},{32,64},{48,80},{64,32},{80,48},{96,0},{112,16},{1... | collective-permute-start | bytes 147464 | tf_op jit(solution)/shard_map/ppermute | solution.py:212
  59.9 7.0 %collective-permute-start.21 = (f32[4,5,8,128]{3,2,1,0:T(8,128)S(1)}, f32[4,5,8,128]{3,2,1,0:T(8,128)S(1)}, u32[]{:S(2)}, u32[]{:S(2)}) collective-permute-start(f32[4,5,8,128]{3,2,1,0:T(8,128)S(1)} %pad_maximum_fusion.1), channel_id=1, source_target_pairs={{0,96},{16,112},{32,64},{48,80},{64,32},{80,48},{96,0},{112,16},{1... | collective-permute-start | bytes 245768 | tf_op jit(solution)/shard_map/ppermute | solution.py:212
  66.1 5.1 %collective-permute-start.18 = (f32[96,128]{1,0:T(8,128)S(1)}, f32[96,128]{1,0:T(8,128)S(1)}, u32[]{:S(2)}, u32[]{:S(2)}) collective-permute-start(f32[96,128]{1,0:T(8,128)S(1)} %add.59.p_ref), channel_id=1, source_target_pairs={{0,32},{16,48},{32,0},{48,16},{64,96},{80,112},{96,64},{112,80},{1... | collective-permute-start | bytes 147464 | tf_op jit(solution)/shard_map/ppermute | solution.py:212

commit v5 on v4

--- a/solution.py
+++ b/solution.py
@@ -111,7 +111,7 @@
 def form_image(own_ref, r1, r2, r3, old_ref, image_ref, a1_ref, a2_ref, a3_ref, a0_ref, mine_ref):
     yh, yl, z = lax.axis_index("yh"), lax.axis_index("yl"), lax.axis_index("z")
     near = own_ref[...] + r1[...]
-    far = r2[:HALF, :] + r3[...]
+    far = r2[...] + r3[:HALF, :]
     h0 = jnp.where(yh == 0, near, far)
     h1 = jnp.where(yh == 0, far, near)
     low = lax.broadcasted_iota(jnp.int32, (HALF, 128), 1) < 64
@@ -122,7 +122,7 @@
     right = jnp.concatenate([left, jnp.concatenate([low, high], axis=0)], axis=1)
     square = dot(left, right, 0, 0, None)
     square = square[:, :NX] + square[:, NX:]
-    other = r2[HALF:HALF + 64, :R1]
+    other = r3[HALF:HALF + 64, :R1]
     own = old_ref[...]
     old = jnp.concatenate([jnp.where(yh == 0, own, other), jnp.where(yh == 0, other, own)], axis=0)
     image_ref[...] = dot(old, square, 0, 0)
@@ -257,7 +257,7 @@
     (packed,) = call(pack_depth, [(ZS, TILES, 8, 128)], *sums, basis_mid)
     mine = lax.all_to_all(packed, "z", 0, 0, tiled=True)
     part, more = call(project_mid, [(HALF, 128), (HALF + 64, 128)], mine, basis_old)
-    near = {m: swap(more if m == 2 else part, ("yh", "yl"), YS, m) for m in (3, 1, 2)}
+    near = {m: swap(more if m == 3 else part, ("yh", "yl"), YS, m) for m in (3, 1, 2)}
     block = (SLOTS, 8, 128)
     image, a1, a2, a3, a0 = call(
         form_image,

time: 74.6 us -> 74.7 us (level)
  no operation moved by 1% of the time
where the time goes in v5:
time: 74.7 us; the launch traced here: 74.6 us
  starting transfers between devices  24.9 us (33%)
  waiting for transfers between devices  23.1 us (31%)
  blocking collectives  16.8 us (22%)
  Pallas kernels  8.83 us (12%)
  between operations  0.78 us (1%)
    ppermute x16, starting transfers between devices, swap(): return lax.ppermute(value, axis, [(i, i ^ bit) for i in range(size)])  19.4 us
    ppermute x16, waiting for transfers between devices, swap(): return lax.ppermute(value, axis, [(i, i ^ bit) for i in range(size)])  19.1 us
    all_to_all x1, blocking collectives, on_device(): mine = lax.all_to_all(packed, 'z', 0, 0, tiled=True)  16.8 us
    pallas_call x6, Pallas kernels, call(): pl.pallas_call(kernel, out_shape=[jax.ShapeDtypeStruct(s, F32) for s in o...  5.81 us
    ppermute x6, starting transfers between devices, across(): lax.ppermute(value, axes, [(i, i ^ m) for i in range(ZS * XS * CORES)])  5.53 us
    ppermute x6, waiting for transfers between devices, across(): lax.ppermute(value, axes, [(i, i ^ m) for i in range(ZS * XS * CORES)])  4.08 us
    pallas_call x1, Pallas kernels, on_device(): pl.pallas_call(project_first, out_shape=[jax.ShapeDtypeStruct(s, F32) for...  1.6 us
  transfers between devices with their start and end apart: 22, of which 12 were waited for; matrix products, arithmetic and copies ran while one was open for 0% of the time, Pallas kernels for 2%

profile of v5, /device:TPU:32, one launch (start us, length us, event | category | flops | bytes accessed | tf_op | source)
XLA Modules:
  0.0 74.6 jit_solution(12921595196448434041)
XLA Ops:
  0.6 1.4 %shard_map.59.cells_ref = f32[3,64,16,128]{3,2,1,0:T(8,128)S(1)} custom-call(f32[6,64,16,128]{3,2,1,0:T(8,128)} %vel_ref.3), custom_call_target="tpu_custom_call" | custom-call | tf_op jit(solution)/shard_map/pallas_call | solution.py:232
  2.1 1.6 %shard_map.60 = (f32[576,128]{1,0:T(8,128)S(1)}, f32[576,128]{1,0:T(8,128)S(1)}, f32[3,64,16,128]{3,2,1,0:T(8,128)S(1)}) custom-call(f32[3,64,16,128]{3,2,1,0:T(8,128)S(1)} %shard_map.59.cells_ref, f32[6,64,16,128]{3,2,1,0:T(8,128)} %vel_ref.3, f32[48,128]{1,0:T(8,128)S(1)} %bitcast.1), custom_call_target="tpu_custom_call" | custom-call | tf_op jit(solution)/shard_map/pallas_call | solution.py:240
  3.7 0.1 collective-permute-start
  3.8 0.0 copy-start.2
  3.8 1.1 %shard_map.61 = (f32[576,128]{1,0:T(8,128)S(1)}, f32[576,128]{1,0:T(8,128)S(1)}) custom-call(f32[3,64,16,128]{3,2,1,0:T(8,128)S(1)} %get-tuple-element.16.cells_ref, f32[48,128]{1,0:T(8,128)S(1)} %bitcast.2), custom_call_target="tpu_custom_call" | custom-call | tf_op jit(solution)/shard_map/pallas_call | solution.py:201
  4.9 0.0 copy-start
  4.9 0.6 collective-permute-start.4
  5.5 0.0 collective-permute-done
  5.6 2.8 %collective-permute-start.3 = (f32[144,128]{1,0:T(8,128)S(1)}, f32[144,128]{1,0:T(8,128)S(1)}, u32[]{:S(2)}, u32[]{:S(2)}) collective-permute-start(f32[144,128]{1,0:T(8,128)S(1)} %get-tuple-element.30), channel_id=1, source_target_pairs={{0,6},{2,4},{4,2},{6,0},{1,7},{3,5},{5,3},{7,1},{8,14},{10,12},{12... | collective-permute-start | bytes 221192 | tf_op jit(solution)/shard_map/ppermute | solution.py:212
  8.4 0.8 %collective-permute-start.2 = (f32[144,128]{1,0:T(8,128)S(1)}, f32[144,128]{1,0:T(8,128)S(1)}, u32[]{:S(2)}, u32[]{:S(2)}) collective-permute-start(f32[144,128]{1,0:T(8,128)S(1)} %get-tuple-element.31), channel_id=1, source_target_pairs={{0,4},{2,6},{4,0},{6,2},{1,5},{3,7},{5,1},{7,3},{8,12},{10,14},{12... | collective-permute-start | bytes 221192 | tf_op jit(solution)/shard_map/ppermute | solution.py:212
  9.2 0.5 collective-permute-start.1
  9.7 0.0 collective-permute-done.4
  9.8 2.8 %collective-permute-start.7 = (f32[144,128]{1,0:T(8,128)S(1)}, f32[144,128]{1,0:T(8,128)S(1)}, u32[]{:S(2)}, u32[]{:S(2)}) collective-permute-start(f32[144,128]{1,0:T(8,128)S(1)} %get-tuple-element.26), channel_id=1, source_target_pairs={{0,6},{2,4},{4,2},{6,0},{1,7},{3,5},{5,3},{7,1},{8,14},{10,12},{12... | collective-permute-start | bytes 221192 | tf_op jit(solution)/shard_map/ppermute | solution.py:212
  12.6 0.8 %collective-permute-start.6 = (f32[144,128]{1,0:T(8,128)S(1)}, f32[144,128]{1,0:T(8,128)S(1)}, u32[]{:S(2)}, u32[]{:S(2)}) collective-permute-start(f32[144,128]{1,0:T(8,128)S(1)} %get-tuple-element.27), channel_id=1, source_target_pairs={{0,4},{2,6},{4,0},{6,2},{1,5},{3,7},{5,1},{7,3},{8,12},{10,14},{12... | collective-permute-start | bytes 221192 | tf_op jit(solution)/shard_map/ppermute | solution.py:212
  13.4 0.5 collective-permute-start.5
  14.0 0.7 collective-permute-done.2.c0
  14.6 0.8 %collective-permute-done.7.d1 = f32[144,128]{1,0:T(8,128)S(1)} collective-permute-done((f32[144,128]{1,0:T(8,128)S(1)}, f32[144,128]{1,0:T(8,128)S(1)}, u32[]{:S(2)}, u32[]{:S(2)}) %collective-permute-start.7) | collective-permute-done | bytes 73760 | tf_op jit(solution)/shard_map/ppermute | solution.py:212
  15.4 3.1 %collective-permute-done.6.c1 = f32[144,128]{1,0:T(8,128)S(1)} collective-permute-done((f32[144,128]{1,0:T(8,128)S(1)}, f32[144,128]{1,0:T(8,128)S(1)}, u32[]{:S(2)}, u32[]{:S(2)}) %collective-permute-start.6) | collective-permute-done | bytes 73760 | tf_op jit(solution)/shard_map/ppermute | solution.py:212
  18.5 0.0 collective-permute-done.5.b1
  18.5 0.2 shard_map.62
  18.7 16.8 %all_to_all.5.got_ref = f32[8,7,8,128]{3,2,1,0:T(8,128)S(1)} all-to-all(f32[8,7,8,128]{3,2,1,0:T(8,128)S(1)} %shard_map.62), channel_id=1, replica_groups=mesh['yh'=2,'z'=8,'yl'=2,'x'=4,'core'=2] {'z'}, dimensions={0} | all-to-all | bytes 458752 | tf_op jit(solution)/shard_map/all_to_all | solution.py:258
  35.5 0.5 shard_map.63
  36.0 3.1 %collective-permute-start.10 = (f32[304,128]{1,0:T(8,128)S(1)}, f32[304,128]{1,0:T(8,128)S(1)}, u32[]{:S(2)}, u32[]{:S(2)}) collective-permute-start(f32[304,128]{1,0:T(8,128)S(1)} %get-tuple-element.20), channel_id=1, source_target_pairs={{0,136},{8,128},{128,8},{136,0},{1,137},{9,129},{129,9},{137,1},{2... | collective-permute-start | bytes 466952 | tf_op jit(solution)/shard_map/ppermute | solution.py:212
  39.1 0.6 collective-permute-start.9
  39.7 0.5 collective-permute-start.8
  40.2 5.3 %collective-permute-done.9.r2 = f32[240,128]{1,0:T(8,128)S(1)} collective-permute-done((f32[240,128]{1,0:T(8,128)S(1)}, f32[240,128]{1,0:T(8,128)S(1)}, u32[]{:S(2)}, u32[]{:S(2)}) %collective-permute-start.9) | collective-permute-done | bytes 122912 | tf_op jit(solution)/shard_map/ppermute | solution.py:212
  45.5 0.6 shard_map.64
  46.1 0.1 collective-permute-start.13
  46.2 1.8 %collective-permute-start.12 = (f32[96,128]{1,0:T(8,128)S(1)}, f32[96,128]{1,0:T(8,128)S(1)}, u32[]{:S(2)}, u32[]{:S(2)}) collective-permute-start(f32[96,128]{1,0:T(8,128)S(1)} %get-tuple-element.21), channel_id=1, source_target_pairs={{0,16},{1,17},{2,18},{3,19},{4,20},{5,21},{6,22},{7,23},{16,0},{17... | collective-permute-start | bytes 147464 | tf_op jit(solution)/shard_map/ppermute | solution.py:218
  48.0 0.1 collective-permute-start.11
  48.0 1.7 %collective-permute-start.19 = (f32[4,5,8,128]{3,2,1,0:T(8,128)S(1)}, f32[4,5,8,128]{3,2,1,0:T(8,128)S(1)}, u32[]{:S(2)}, u32[]{:S(2)}) collective-permute-start(f32[4,5,8,128]{3,2,1,0:T(8,128)S(1)} %get-tuple-element.23), channel_id=1, source_target_pairs={{0,16},{16,0},{32,48},{48,32},{64,80},{80,64},{96,112},{112,96},{1... | collective-permute-start | bytes 245768 | tf_op jit(solution)/shard_map/ppermute | solution.py:212
  49.7 0.2 collective-permute-done.13
  49.9 0.9 %collective-permute-done.12 = f32[96,128]{1,0:T(8,128)S(1)} collective-permute-done((f32[96,128]{1,0:T(8,128)S(1)}, f32[96,128]{1,0:T(8,128)S(1)}, u32[]{:S(2)}, u32[]{:S(2)}) %collective-permute-start.12) | collective-permute-done | bytes 49184 | tf_op jit(solution)/shard_map/ppermute | solution.py:218
  50.9 2.1 %collective-permute-start.16 = (f32[96,128]{1,0:T(8,128)S(1)}, f32[96,128]{1,0:T(8,128)S(1)}, u32[]{:S(2)}, u32[]{:S(2)}) collective-permute-start(f32[96,128]{1,0:T(8,128)S(1)} %add_add_fusion.1), channel_id=1, source_target_pairs={{0,4},{1,5},{2,6},{3,7},{4,0},{5,1},{6,2},{7,3},{16,20},{17,21},{1... | collective-permute-start | bytes 147464 | tf_op jit(solution)/shard_map/ppermute | solution.py:218
  53.0 0.8 %collective-permute-start.15 = (f32[96,128]{1,0:T(8,128)S(1)}, f32[96,128]{1,0:T(8,128)S(1)}, u32[]{:S(2)}, u32[]{:S(2)}) collective-permute-start(f32[96,128]{1,0:T(8,128)S(1)} %add_add_fusion.1), channel_id=1, source_target_pairs={{0,6},{1,7},{2,4},{3,5},{4,2},{5,3},{6,0},{7,1},{16,22},{17,23},{1... | collective-permute-start | bytes 147464 | tf_op jit(solution)/shard_map/ppermute | solution.py:218
  53.9 0.6 collective-permute-start.14
  54.5 0.9 %collective-permute-start.20 = (f32[4,5,8,128]{3,2,1,0:T(8,128)S(1)}, f32[4,5,8,128]{3,2,1,0:T(8,128)S(1)}, u32[]{:S(2)}, u32[]{:S(2)}) collective-permute-start(f32[4,5,8,128]{3,2,1,0:T(8,128)S(1)} %pad_maximum_fusion), channel_id=1, source_target_pairs={{0,32},{16,48},{32,0},{48,16},{64,96},{80,112},{96,64},{112,80},{1... | collective-permute-start | bytes 245768 | tf_op jit(solution)/shard_map/ppermute | solution.py:212
  55.4 1.2 %collective-permute-done.16 = f32[96,128]{1,0:T(8,128)S(1)} collective-permute-done((f32[96,128]{1,0:T(8,128)S(1)}, f32[96,128]{1,0:T(8,128)S(1)}, u32[]{:S(2)}, u32[]{:S(2)}) %collective-permute-start.16) | collective-permute-done | bytes 49184 | tf_op jit(solution)/shard_map/ppermute | solution.py:218
  56.6 1.8 %collective-permute-done.15 = f32[96,128]{1,0:T(8,128)S(1)} collective-permute-done((f32[96,128]{1,0:T(8,128)S(1)}, f32[96,128]{1,0:T(8,128)S(1)}, u32[]{:S(2)}, u32[]{:S(2)}) %collective-permute-start.15) | collective-permute-done | bytes 49184 | tf_op jit(solution)/shard_map/ppermute | solution.py:218
  58.3 0.9 %collective-permute-start.17 = (f32[96,128]{1,0:T(8,128)S(1)}, f32[96,128]{1,0:T(8,128)S(1)}, u32[]{:S(2)}, u32[]{:S(2)}) collective-permute-start(f32[96,128]{1,0:T(8,128)S(1)} %add_add_fusion), channel_id=1, source_target_pairs={{0,96},{16,112},{32,64},{48,80},{64,32},{80,48},{96,0},{112,16},{1... | collective-permute-start | bytes 147464 | tf_op jit(solution)/shard_map/ppermute | solution.py:212
  59.2 0.8 %collective-permute-done.20.r2_ref = f32[4,5,8,128]{3,2,1,0:T(8,128)S(1)} collective-permute-done((f32[4,5,8,128]{3,2,1,0:T(8,128)S(1)}, f32[4,5,8,128]{3,2,1,0:T(8,128)S(1)}, u32[]{:S(2)}, u32[]{:S(2)}) %collective-permute-start.20) | collective-permute-done | bytes 81952 | tf_op jit(solution)/shard_map/ppermute | solution.py:212
  60.0 2.6 %collective-permute-start.21 = (f32[4,5,8,128]{3,2,1,0:T(8,128)S(1)}, f32[4,5,8,128]{3,2,1,0:T(8,128)S(1)}, u32[]{:S(2)}, u32[]{:S(2)}) collective-permute-start(f32[4,5,8,128]{3,2,1,0:T(8,128)S(1)} %pad_maximum_fusion.1), channel_id=1, source_target_pairs={{0,96},{16,112},{32,64},{48,80},{64,32},{80,48},{96,0},{112,16},{1... | collective-permute-start | bytes 245768 | tf_op jit(solution)/shard_map/ppermute | solution.py:212
  62.7 3.5 %collective-permute-done.17 = f32[96,128]{1,0:T(8,128)S(1)} collective-permute-done((f32[96,128]{1,0:T(8,128)S(1)}, f32[96,128]{1,0:T(8,128)S(1)}, u32[]{:S(2)}, u32[]{:S(2)}) %collective-permute-start.17) | collective-permute-done | bytes 49184 | tf_op jit(solution)/shard_map/ppermute | solution.py:212
  66.2 0.1 collective-permute-start.18
  66.3 0.8 %collective-permute-done.21.r3_ref = f32[4,5,8,128]{3,2,1,0:T(8,128)S(1)} collective-permute-done((f32[4,5,8,128]{3,2,1,0:T(8,128)S(1)}, f32[4,5,8,128]{3,2,1,0:T(8,128)S(1)}, u32[]{:S(2)}, u32[]{:S(2)}) %collective-permute-start.21) | collective-permute-done | bytes 81952 | tf_op jit(solution)/shard_map/ppermute | solution.py:212
  67.1 0.1 shard_map.65.rows_ref
  67.2 4.1 %collective-permute-done.18.q_ref = f32[96,128]{1,0:T(8,128)S(1)} collective-permute-done((f32[96,128]{1,0:T(8,128)S(1)}, f32[96,128]{1,0:T(8,128)S(1)}, u32[]{:S(2)}, u32[]{:S(2)}) %collective-permute-start.18) | collective-permute-done | bytes 49184 | tf_op jit(solution)/shard_map/ppermute | solution.py:212
  71.3 3.3 %shard_map.66 = (f32[64,96]{1,0:T(8,128)}, f32[6,6,6,96]{3,2,1,0:T(8,128)}) custom-call(f32[96,128]{1,0:T(8,128)S(1)} %add.59.p_ref, f32[96,128]{1,0:T(8,128)S(1)} %collective-permute-done.18.q_ref, f32[288,128]{1,0:T(8,128)S(1)} %shard_map.65.rows_ref), custom_call_target="tpu_custom_call" | custom-call | tf_op jit(solution)/shard_map/pallas_call | solution.py:201
  (21 shorter events, 0.1 us)
Async XLA Ops:
  0.6 1.4 %copy-start.1 = (f32[128,48]{0,1:T(8,128)S(1)}, f32[128,48]{0,1:T(8,128)}, u32[]{:S(2)}) copy-start(f32[128,48]{0,1:T(8,128)} %param.7) | copy-start | bytes 73732
  3.7 1.8 %collective-permute-start = (f32[576,128]{1,0:T(8,128)S(1)}, f32[576,128]{1,0:T(8,128)S(1)}, u32[]{:S(2)}, u32[]{:S(2)}) collective-permute-start(f32[576,128]{1,0:T(8,128)S(1)} %get-tuple-element.15), channel_id=1, source_target_pairs={{0,1},{1,0},{2,3},{3,2},{4,5},{5,4},{6,7},{7,6},{8,9},{9,8},{10,11... | collective-permute-start | bytes 884744 | tf_op jit(solution)/shard_map/ppermute | solution.py:212
  3.8 14.7 %copy-start.2 = (f32[16,96]{1,0:T(8,128)S(1)}, f32[16,96]{1,0:T(8,128)}, u32[]{:S(2)}) copy-start(f32[16,96]{1,0:T(8,128)} %mid_ref.1) | copy-start | bytes 18436
  4.9 30.6 %copy-start = (f32[64,96]{1,0:T(8,128)S(1)}, f32[64,96]{1,0:T(8,128)}, u32[]{:S(2)}) copy-start(f32[64,96]{1,0:T(8,128)} %old_ref.3) | copy-start | bytes 73732
  4.9 4.8 %collective-permute-start.4 = (f32[576,128]{1,0:T(8,128)S(1)}, f32[576,128]{1,0:T(8,128)S(1)}, u32[]{:S(2)}, u32[]{:S(2)}) collective-permute-start(f32[576,128]{1,0:T(8,128)S(1)} %get-tuple-element.18), channel_id=1, source_target_pairs={{0,1},{1,0},{2,3},{3,2},{4,5},{5,4},{6,7},{7,6},{8,9},{9,8},{10,11... | collective-permute-start | bytes 884744 | tf_op jit(solution)/shard_map/ppermute | solution.py:212
  5.6 7.9 %collective-permute-start.3 = (f32[144,128]{1,0:T(8,128)S(1)}, f32[144,128]{1,0:T(8,128)S(1)}, u32[]{:S(2)}, u32[]{:S(2)}) collective-permute-start(f32[144,128]{1,0:T(8,128)S(1)} %get-tuple-element.30), channel_id=1, source_target_pairs={{0,6},{2,4},{4,2},{6,0},{1,7},{3,5},{5,3},{7,1},{8,14},{10,12},{12... | collective-permute-start | bytes 221192 | tf_op jit(solution)/shard_map/ppermute | solution.py:212
  8.4 6.2 %collective-permute-start.2 = (f32[144,128]{1,0:T(8,128)S(1)}, f32[144,128]{1,0:T(8,128)S(1)}, u32[]{:S(2)}, u32[]{:S(2)}) collective-permute-start(f32[144,128]{1,0:T(8,128)S(1)} %get-tuple-element.31), channel_id=1, source_target_pairs={{0,4},{2,6},{4,0},{6,2},{1,5},{3,7},{5,1},{7,3},{8,12},{10,14},{12... | collective-permute-start | bytes 221192 | tf_op jit(solution)/shard_map/ppermute | solution.py:212
  9.2 5.4 %collective-permute-start.1 = (f32[144,128]{1,0:T(8,128)S(1)}, f32[144,128]{1,0:T(8,128)S(1)}, u32[]{:S(2)}, u32[]{:S(2)}) collective-permute-start(f32[144,128]{1,0:T(8,128)S(1)} %get-tuple-element.32), channel_id=1, source_target_pairs={{0,2},{2,0},{4,6},{6,4},{1,3},{3,1},{5,7},{7,5},{8,10},{10,8},{12,... | collective-permute-start | bytes 221192 | tf_op jit(solution)/shard_map/ppermute | solution.py:212
  9.8 5.7 %collective-permute-start.7 = (f32[144,128]{1,0:T(8,128)S(1)}, f32[144,128]{1,0:T(8,128)S(1)}, u32[]{:S(2)}, u32[]{:S(2)}) collective-permute-start(f32[144,128]{1,0:T(8,128)S(1)} %get-tuple-element.26), channel_id=1, source_target_pairs={{0,6},{2,4},{4,2},{6,0},{1,7},{3,5},{5,3},{7,1},{8,14},{10,12},{12... | collective-permute-start | bytes 221192 | tf_op jit(solution)/shard_map/ppermute | solution.py:212
  12.6 5.9 %collective-permute-start.6 = (f32[144,128]{1,0:T(8,128)S(1)}, f32[144,128]{1,0:T(8,128)S(1)}, u32[]{:S(2)}, u32[]{:S(2)}) collective-permute-start(f32[144,128]{1,0:T(8,128)S(1)} %get-tuple-element.27), channel_id=1, source_target_pairs={{0,4},{2,6},{4,0},{6,2},{1,5},{3,7},{5,1},{7,3},{8,12},{10,14},{12... | collective-permute-start | bytes 221192 | tf_op jit(solution)/shard_map/ppermute | solution.py:212
  13.4 5.1 %collective-permute-start.5 = (f32[144,128]{1,0:T(8,128)S(1)}, f32[144,128]{1,0:T(8,128)S(1)}, u32[]{:S(2)}, u32[]{:S(2)}) collective-permute-start(f32[144,128]{1,0:T(8,128)S(1)} %get-tuple-element.28), channel_id=1, source_target_pairs={{0,2},{2,0},{4,6},{6,4},{1,3},{3,1},{5,7},{7,5},{8,10},{10,8},{12,... | collective-permute-start | bytes 221192 | tf_op jit(solution)/shard_map/ppermute | solution.py:212
  36.0 9.5 %collective-permute-start.10 = (f32[304,128]{1,0:T(8,128)S(1)}, f32[304,128]{1,0:T(8,128)S(1)}, u32[]{:S(2)}, u32[]{:S(2)}) collective-permute-start(f32[304,128]{1,0:T(8,128)S(1)} %get-tuple-element.20), channel_id=1, source_target_pairs={{0,136},{8,128},{128,8},{136,0},{1,137},{9,129},{129,9},{137,1},{2... | collective-permute-start | bytes 466952 | tf_op jit(solution)/shard_map/ppermute | solution.py:212
  39.1 6.4 %collective-permute-start.9 = (f32[240,128]{1,0:T(8,128)S(1)}, f32[240,128]{1,0:T(8,128)S(1)}, u32[]{:S(2)}, u32[]{:S(2)}) collective-permute-start(f32[240,128]{1,0:T(8,128)S(1)} %get-tuple-element.19.own_ref), channel_id=1, source_target_pairs={{0,128},{8,136},{128,0},{136,8},{1,129},{9,137},{129,1},{137,9},{2... | collective-permute-start | bytes 368648 | tf_op jit(solution)/shard_map/ppermute | solution.py:212
  39.7 5.8 %collective-permute-start.8 = (f32[240,128]{1,0:T(8,128)S(1)}, f32[240,128]{1,0:T(8,128)S(1)}, u32[]{:S(2)}, u32[]{:S(2)}) collective-permute-start(f32[240,128]{1,0:T(8,128)S(1)} %get-tuple-element.19.own_ref), channel_id=1, source_target_pairs={{0,8},{8,0},{128,136},{136,128},{1,9},{9,1},{129,137},{137,129},{2... | collective-permute-start | bytes 368648 | tf_op jit(solution)/shard_map/ppermute | solution.py:212
  46.1 3.9 %collective-permute-start.13 = (f32[96,128]{1,0:T(8,128)S(1)}, f32[96,128]{1,0:T(8,128)S(1)}, u32[]{:S(2)}, u32[]{:S(2)}) collective-permute-start(f32[96,128]{1,0:T(8,128)S(1)} %get-tuple-element.21), channel_id=1, source_target_pairs={{0,17},{1,16},{2,19},{3,18},{4,21},{5,20},{6,23},{7,22},{16,1},{17... | collective-permute-start | bytes 147464 | tf_op jit(solution)/shard_map/ppermute | solution.py:218
  46.2 4.7 %collective-permute-start.12 = (f32[96,128]{1,0:T(8,128)S(1)}, f32[96,128]{1,0:T(8,128)S(1)}, u32[]{:S(2)}, u32[]{:S(2)}) collective-permute-start(f32[96,128]{1,0:T(8,128)S(1)} %get-tuple-element.21), channel_id=1, source_target_pairs={{0,16},{1,17},{2,18},{3,19},{4,20},{5,21},{6,22},{7,23},{16,0},{17... | collective-permute-start | bytes 147464 | tf_op jit(solution)/shard_map/ppermute | solution.py:218
  48.0 2.9 %collective-permute-start.11 = (f32[96,128]{1,0:T(8,128)S(1)}, f32[96,128]{1,0:T(8,128)S(1)}, u32[]{:S(2)}, u32[]{:S(2)}) collective-permute-start(f32[96,128]{1,0:T(8,128)S(1)} %get-tuple-element.21), channel_id=1, source_target_pairs={{0,1},{1,0},{2,3},{3,2},{4,5},{5,4},{6,7},{7,6},{16,17},{17,16},{1... | collective-permute-start | bytes 147464 | tf_op jit(solution)/shard_map/ppermute | solution.py:218
  48.0 6.4 %collective-permute-start.19 = (f32[4,5,8,128]{3,2,1,0:T(8,128)S(1)}, f32[4,5,8,128]{3,2,1,0:T(8,128)S(1)}, u32[]{:S(2)}, u32[]{:S(2)}) collective-permute-start(f32[4,5,8,128]{3,2,1,0:T(8,128)S(1)} %get-tuple-element.23), channel_id=1, source_target_pairs={{0,16},{16,0},{32,48},{48,32},{64,80},{80,64},{96,112},{112,96},{1... | collective-permute-start | bytes 245768 | tf_op jit(solution)/shard_map/ppermute | solution.py:212
  50.9 5.7 %collective-permute-start.16 = (f32[96,128]{1,0:T(8,128)S(1)}, f32[96,128]{1,0:T(8,128)S(1)}, u32[]{:S(2)}, u32[]{:S(2)}) collective-permute-start(f32[96,128]{1,0:T(8,128)S(1)} %add_add_fusion.1), channel_id=1, source_target_pairs={{0,4},{1,5},{2,6},{3,7},{4,0},{5,1},{6,2},{7,3},{16,20},{17,21},{1... | collective-permute-start | bytes 147464 | tf_op jit(solution)/shard_map/ppermute | solution.py:218
  53.0 5.3 %collective-permute-start.15 = (f32[96,128]{1,0:T(8,128)S(1)}, f32[96,128]{1,0:T(8,128)S(1)}, u32[]{:S(2)}, u32[]{:S(2)}) collective-permute-start(f32[96,128]{1,0:T(8,128)S(1)} %add_add_fusion.1), channel_id=1, source_target_pairs={{0,6},{1,7},{2,4},{3,5},{4,2},{5,3},{6,0},{7,1},{16,22},{17,23},{1... | collective-permute-start | bytes 147464 | tf_op jit(solution)/shard_map/ppermute | solution.py:218
  53.9 4.5 %collective-permute-start.14 = (f32[96,128]{1,0:T(8,128)S(1)}, f32[96,128]{1,0:T(8,128)S(1)}, u32[]{:S(2)}, u32[]{:S(2)}) collective-permute-start(f32[96,128]{1,0:T(8,128)S(1)} %add_add_fusion.1), channel_id=1, source_target_pairs={{0,2},{1,3},{2,0},{3,1},{4,6},{5,7},{6,4},{7,5},{16,18},{17,19},{1... | collective-permute-start | bytes 147464 | tf_op jit(solution)/shard_map/ppermute | solution.py:218
  54.5 5.5 %collective-permute-start.20 = (f32[4,5,8,128]{3,2,1,0:T(8,128)S(1)}, f32[4,5,8,128]{3,2,1,0:T(8,128)S(1)}, u32[]{:S(2)}, u32[]{:S(2)}) collective-permute-start(f32[4,5,8,128]{3,2,1,0:T(8,128)S(1)} %pad_maximum_fusion), channel_id=1, source_target_pairs={{0,32},{16,48},{32,0},{48,16},{64,96},{80,112},{96,64},{112,80},{1... | collective-permute-start | bytes 245768 | tf_op jit(solution)/shard_map/ppermute | solution.py:212
  58.3 7.8 %collective-permute-start.17 = (f32[96,128]{1,0:T(8,128)S(1)}, f32[96,128]{1,0:T(8,128)S(1)}, u32[]{:S(2)}, u32[]{:S(2)}) collective-permute-start(f32[96,128]{1,0:T(8,128)S(1)} %add_add_fusion), channel_id=1, source_target_pairs={{0,96},{16,112},{32,64},{48,80},{64,32},{80,48},{96,0},{112,16},{1... | collective-permute-start | bytes 147464 | tf_op jit(solution)/shard_map/ppermute | solution.py:212
  60.0 7.0 %collective-permute-start.21 = (f32[4,5,8,128]{3,2,1,0:T(8,128)S(1)}, f32[4,5,8,128]{3,2,1,0:T(8,128)S(1)}, u32[]{:S(2)}, u32[]{:S(2)}) collective-permute-start(f32[4,5,8,128]{3,2,1,0:T(8,128)S(1)} %pad_maximum_fusion.1), channel_id=1, source_target_pairs={{0,96},{16,112},{32,64},{48,80},{64,32},{80,48},{96,0},{112,16},{1... | collective-permute-start | bytes 245768 | tf_op jit(solution)/shard_map/ppermute | solution.py:212
  66.2 5.1 %collective-permute-start.18 = (f32[96,128]{1,0:T(8,128)S(1)}, f32[96,128]{1,0:T(8,128)S(1)}, u32[]{:S(2)}, u32[]{:S(2)}) collective-permute-start(f32[96,128]{1,0:T(8,128)S(1)} %add.59.p_ref), channel_id=1, source_target_pairs={{0,32},{16,48},{32,0},{48,16},{64,96},{80,112},{96,64},{112,80},{1... | collective-permute-start | bytes 147464 | tf_op jit(solution)/shard_map/ppermute | solution.py:212
